TPU v7x, 32 devices: a whole 2x2x4 slice. The times are simulated.
32 devices in a mesh: seq: 4 (over y, x), batch: 8 (over z, core).
Axes of the slice: x: 2, y: 2, z: 4, core: 2. Of those that a mesh axis runs over, the one named last changes fastest.
Arguments:
- hidden_in: bfloat16 [8, 1536, 512], P('batch', 'seq'), may hold values from -6 to 6
- out_grad: bfloat16 [8, 1536, 512], P('batch', 'seq'), may hold values from -6 to 6
- start_flags: int32 [8, 1536], P('batch', 'seq'), may hold values 0 or 1
- ln_gain: bfloat16 [2, 2, 512], replicated, may hold values from 0.5 to 1.5
- ln_bias: bfloat16 [2, 2, 512], replicated, may hold values from -1.5 to 1.5
- w_qkv: bfloat16 [2, 512, 1536], replicated, may hold values from -0.25 to 0.25
- w_out: bfloat16 [2, 512, 512], replicated, may hold values from -0.75 to 0.75
- slopes: float32 [2, 8], replicated, may hold values from 0.00032552084 to 0.1
- w_in: bfloat16 [2, 512, 2048], replicated, may hold values from -0.25 to 0.25
- b_in: bfloat16 [2, 2048], replicated, may hold values from -1.5 to 1.5
- w_back: bfloat16 [2, 2048, 512], replicated, may hold values from -0.125 to 0.125
- b_back: bfloat16 [2, 512], replicated, may hold values from -1.5 to 1.5
- w_pool: bfloat16 [1536, 512], replicated, may hold values from -0.15625 to 0.15625
- b_pool: bfloat16 [512], replicated, may hold values from -1.5 to 1.5
- w_up: bfloat16 [512, 1536], replicated, may hold values from -0.25 to 0.25
- b_up: bfloat16 [1536], replicated, may hold values from -1.5 to 1.5
Outputs:
- block_out: bfloat16 [8, 1536, 512], P('batch', 'seq')
- hidden_grad: float32 [8, 1536, 512], P('batch', 'seq')
- ln_gain_grad: float32 [2, 2, 512], P(None, None, 'batch')
- ln_bias_grad: float32 [2, 2, 512], P(None, None, 'batch')
- w_qkv_grad: float32 [2, 512, 1536], P(None, None, 'batch')
- w_out_grad: float32 [2, 512, 512], P(None, None, 'batch')
- slopes_grad: float32 [2, 8], replicated
- w_in_grad: float32 [2, 512, 2048], P(None, None, 'batch')
- b_in_grad: float32 [2, 2048], P(None, 'batch')
- w_back_grad: float32 [2, 2048, 512], P(None, None, 'batch')
- b_back_grad: float32 [2, 512], P(None, 'batch')
- w_pool_grad: float32 [1536, 512], P(None, 'batch')
- b_pool_grad: float32 [512], P('batch')
- w_up_grad: float32 [512, 1536], P(None, 'batch')
- b_up_grad: float32 [1536], P('batch')
All inputs are finite; a program needn't handle non-finite values. No bound on the sum of `start_flags` on one device may be relied on, other than what follows from the above.
Results may differ from a plain program's by a relative error of at most 0.028.
Values may be sent and summed in bfloat16 or wider, within the bound.
No kernel may reach another device: no remote copies, remote signals or barrier semaphores. Data moves between devices by JAX's collectives and lax.ppermute only.
A program may use at most 192 MiB of HBM per device.

v0:
```python
import jax
import jax.numpy as jnp
from jax import lax
from jax.sharding import PartitionSpec as P

EPSILON = 1e-05
NEGATIVE = -1e30


def shifted(shard, axis, by):
    count = lax.axis_size(axis)
    pairs = [(i, i + by) for i in range(count) if 0 <= i + by < count]
    return lax.ppermute(shard, axis, pairs)


def for_sending(shard):
    return jax.tree.map(lambda a: a.astype(jnp.bfloat16) if a.dtype == jnp.float32 else a, shard)


def normalize(values_in, gain_row, bias_row):
    row_mean = jnp.mean(values_in, axis=-1, keepdims=True)
    centred = values_in - row_mean
    spread = jnp.mean(centred * centred, axis=-1, keepdims=True)
    return centred * lax.rsqrt(spread + EPSILON) * gain_row + bias_row


def block_scores(query_heads, key_heads, query_start, key_start, slope_row):
    row_count = query_heads.shape[0]
    column_count = key_heads.shape[0]
    score_scale = query_heads.shape[2] ** (-0.5)
    raw_scores = (
        jnp.einsum("qhe,khe->hqk", query_heads, key_heads, preferred_element_type=jnp.float32)
        * score_scale
    )
    query_pos = query_start + lax.broadcasted_iota(jnp.int32, (row_count, column_count), 0)
    key_pos = key_start + lax.broadcasted_iota(jnp.int32, (row_count, column_count), 1)
    distance = (query_pos - key_pos).astype(jnp.float32)
    scores = raw_scores - slope_row[:, None, None] * distance[None]
    return (jnp.where(distance[None] >= 0, scores, NEGATIVE), distance)


def split_block(key_value, block, row_count, head_count):
    model_width = key_value.shape[1] // 2
    head_size = model_width // head_count
    rows_here = lax.dynamic_slice_in_dim(key_value, block * row_count, row_count, 0)
    key_heads = rows_here[:, :model_width].reshape(row_count, head_count, head_size)
    value_heads = rows_here[:, model_width:].reshape(row_count, head_count, head_size)
    return (key_heads, value_heads)


def attend_forward(query_rows, key_value, slope_row, seq_index):
    row_count, model_width = query_rows.shape
    head_count = slope_row.shape[0]
    head_size = model_width // head_count
    query_heads = query_rows.reshape(row_count, head_count, head_size)
    query_start = seq_index * row_count

    def stats_step(block, state_now):
        row_top, row_total = state_now
        key_heads, _ = split_block(key_value, block, row_count, head_count)
        scores, _ = block_scores(query_heads, key_heads, query_start, block * row_count, slope_row)
        new_top = jnp.maximum(row_top, jnp.max(scores, axis=2))
        row_total = row_total * jnp.exp(row_top - new_top) + jnp.sum(
            jnp.exp(scores - new_top[:, :, None]), axis=2
        )
        return (new_top, row_total)

    start_state = (
        jnp.full((head_count, row_count), NEGATIVE, jnp.float32),
        jnp.zeros((head_count, row_count), jnp.float32),
    )
    row_top, row_total = lax.fori_loop(0, seq_index + 1, stats_step, start_state)
    log_total = row_top + jnp.log(row_total)

    def output_step(block, accum):
        key_heads, value_heads = split_block(key_value, block, row_count, head_count)
        scores, _ = block_scores(query_heads, key_heads, query_start, block * row_count, slope_row)
        soft_weights = jnp.exp(scores - log_total[:, :, None]).astype(jnp.bfloat16)
        return accum + jnp.einsum(
            "hqk,khe->qhe", soft_weights, value_heads, preferred_element_type=jnp.float32
        )

    accum = lax.fori_loop(
        0, seq_index + 1, output_step, jnp.zeros((row_count, head_count, head_size), jnp.float32)
    )
    return (accum.reshape(row_count, model_width), log_total)


def attend_backward(query_rows, key_value, slope_row, log_total, row_terms, mixed_grad, seq_index):
    row_count, model_width = query_rows.shape
    head_count = slope_row.shape[0]
    head_size = model_width // head_count
    score_scale = head_size ** (-0.5)
    query_heads = query_rows.reshape(row_count, head_count, head_size)
    grad_heads = mixed_grad.reshape(row_count, head_count, head_size)
    query_start = seq_index * row_count

    def grad_step(block, state_now):
        grad_query, grad_keys, grad_slope = state_now
        key_heads, value_heads = split_block(key_value, block, row_count, head_count)
        scores, distance = block_scores(
            query_heads, key_heads, query_start, block * row_count, slope_row
        )
        soft_weights = jnp.exp(scores - log_total[:, :, None])
        weight_grads = jnp.einsum(
            "qhe,khe->hqk", grad_heads, value_heads, preferred_element_type=jnp.float32
        )
        score_grads = (soft_weights * (weight_grads - row_terms[:, :, None])).astype(jnp.bfloat16)
        grad_query = grad_query + jnp.einsum(
            "hqk,khe->qhe", score_grads, key_heads, preferred_element_type=jnp.float32
        )
        key_part = jnp.einsum(
            "hqk,qhe->khe", score_grads, query_heads, preferred_element_type=jnp.float32
        )
        value_part = jnp.einsum(
            "hqk,qhe->khe",
            soft_weights.astype(jnp.bfloat16),
            grad_heads,
            preferred_element_type=jnp.float32,
        )
        piece = jnp.concatenate(
            [
                key_part.reshape(row_count, model_width) * score_scale,
                value_part.reshape(row_count, model_width),
            ],
            axis=1,
        )
        current = lax.dynamic_slice_in_dim(grad_keys, block * row_count, row_count, 0)
        grad_keys = lax.dynamic_update_slice_in_dim(
            grad_keys, current + piece, block * row_count, 0
        )
        grad_slope = grad_slope - jnp.sum(
            score_grads.astype(jnp.float32) * distance[None], axis=(1, 2)
        )
        return (grad_query, grad_keys, grad_slope)

    start_state = (
        jnp.zeros((row_count, head_count, head_size), jnp.float32),
        jnp.zeros(key_value.shape, jnp.float32),
        jnp.zeros((head_count,), jnp.float32),
    )
    grad_query, grad_keys, grad_slope = lax.fori_loop(0, seq_index + 1, grad_step, start_state)
    return (grad_query.reshape(row_count, model_width) * score_scale, grad_keys, grad_slope)


def layer_weights(which, ln_gain, ln_bias, w_qkv, w_out, slopes, w_in, b_in, w_back, b_back):
    return (
        ln_gain[which].astype(jnp.float32),
        ln_bias[which].astype(jnp.float32),
        w_qkv[which],
        w_out[which],
        slopes[which],
        w_in[which],
        b_in[which].astype(jnp.float32),
        w_back[which],
        b_back[which].astype(jnp.float32),
    )


def layer_forward(values_in, weights, seq_index, fetch_keys):
    gain_rows, bias_rows, w_qkv, w_out, slope_row, w_in, b_in, w_back, b_back = weights
    model_width = values_in.shape[1]
    attn_in = normalize(values_in, gain_rows[0], bias_rows[0]).astype(jnp.bfloat16)
    qkv_rows = jnp.dot(attn_in, w_qkv, preferred_element_type=jnp.float32).astype(jnp.bfloat16)
    key_value = fetch_keys(qkv_rows[:, model_width:])
    mixed, log_total = attend_forward(qkv_rows[:, :model_width], key_value, slope_row, seq_index)
    mixed_low = mixed.astype(jnp.bfloat16)
    middle = values_in + jnp.dot(mixed_low, w_out, preferred_element_type=jnp.float32)
    ffn_in = normalize(middle, gain_rows[1], bias_rows[1]).astype(jnp.bfloat16)
    pre_act = jnp.dot(ffn_in, w_in, preferred_element_type=jnp.float32) + b_in
    activated = jax.nn.gelu(pre_act).astype(jnp.bfloat16)
    result = middle + jnp.dot(activated, w_back, preferred_element_type=jnp.float32) + b_back
    stored = (
        attn_in,
        qkv_rows,
        key_value,
        log_total,
        mixed,
        mixed_low,
        middle,
        ffn_in,
        pre_act,
        activated,
    )
    return (result, stored)


def layer_backward(values_in, weights, stored, grad_out, seq_index, refetch, send_back):
    gain_rows, bias_rows, w_qkv, w_out, slope_row, w_in, b_in, w_back, b_back = weights
    (
        attn_in,
        qkv_rows,
        key_value,
        log_total,
        mixed,
        mixed_low,
        middle,
        ffn_in,
        pre_act,
        activated,
    ) = stored
    row_count, model_width = values_in.shape
    head_count = slope_row.shape[0]
    head_size = model_width // head_count
    branch_grad = grad_out.astype(jnp.bfloat16)
    back_grad = jnp.einsum("rf,rd->fd", activated, branch_grad, preferred_element_type=jnp.float32)
    back_bias_grad = jnp.sum(branch_grad.astype(jnp.float32), axis=0)
    act_grad = jnp.einsum("rd,fd->rf", branch_grad, w_back, preferred_element_type=jnp.float32)
    _, gelu_pull = jax.vjp(jax.nn.gelu, pre_act)
    pre_grad = gelu_pull(act_grad)[0].astype(jnp.bfloat16)
    in_grad = jnp.einsum("rd,rf->df", ffn_in, pre_grad, preferred_element_type=jnp.float32)
    in_bias_grad = jnp.sum(pre_grad.astype(jnp.float32), axis=0)
    ffn_in_grad = jnp.einsum("rf,df->rd", pre_grad, w_in, preferred_element_type=jnp.float32)
    _, late_pull = jax.vjp(normalize, middle, gain_rows[1], bias_rows[1])
    middle_grad, gain_late, bias_late = late_pull(ffn_in_grad)
    middle_grad = middle_grad + grad_out
    attn_branch = middle_grad.astype(jnp.bfloat16)
    out_weight_grad = jnp.einsum(
        "rd,re->de", mixed_low, attn_branch, preferred_element_type=jnp.float32
    )
    mixed_grad = jnp.einsum(
        "re,de->rd", attn_branch, w_out, preferred_element_type=jnp.float32
    ).astype(jnp.bfloat16)
    row_terms = jnp.einsum(
        "qhe,qhe->hq",
        mixed_grad.reshape(row_count, head_count, head_size).astype(jnp.float32),
        mixed.reshape(row_count, head_count, head_size),
    )
    key_value = refetch(qkv_rows, key_value)
    query_rows = qkv_rows[:, :model_width]
    query_grad, key_value_grad, slope_grad = attend_backward(
        query_rows, key_value, slope_row, log_total, row_terms, mixed_grad, seq_index
    )
    own_grad = send_back(key_value_grad)
    qkv_grad = jnp.concatenate([query_grad, own_grad], axis=1).astype(jnp.bfloat16)
    qkv_weight_grad = jnp.einsum("rd,re->de", attn_in, qkv_grad, preferred_element_type=jnp.float32)
    attn_in_grad = jnp.einsum("re,de->rd", qkv_grad, w_qkv, preferred_element_type=jnp.float32)
    _, early_pull = jax.vjp(normalize, values_in, gain_rows[0], bias_rows[0])
    input_grad, gain_early, bias_early = early_pull(attn_in_grad)
    input_grad = input_grad + middle_grad
    grads = (
        jnp.stack([gain_early, gain_late]),
        jnp.stack([bias_early, bias_late]),
        qkv_weight_grad,
        out_weight_grad,
        slope_grad,
        in_grad,
        in_bias_grad,
        back_grad,
        back_bias_grad,
    )
    return (input_grad, grads)


def layer_parts(grads):
    return (grads[0], grads[1], grads[2], grads[3], grads[5], grads[6], grads[7], grads[8])


def keep_keys(qkv_rows, key_value):
    return key_value


def local(
    hidden_in,
    out_grad,
    start_flags,
    ln_gain,
    ln_bias,
    w_qkv,
    w_out,
    slopes,
    w_in,
    b_in,
    w_back,
    b_back,
    w_pool,
    b_pool,
    w_up,
    b_up,
):
    seq_index = lax.axis_index("seq")
    model_width = hidden_in.shape[2]
    full_weights = layer_weights(
        0, ln_gain, ln_bias, w_qkv, w_out, slopes, w_in, b_in, w_back, b_back
    )
    short_weights = layer_weights(
        1, ln_gain, ln_bias, w_qkv, w_out, slopes, w_in, b_in, w_back, b_back
    )
    values_in = hidden_in[0].astype(jnp.float32)
    row_count = values_in.shape[0]

    def fetch_full(key_rows):
        return lax.all_gather(key_rows, "seq", axis=0, tiled=True)

    def fetch_short(key_rows):
        return lax.all_gather(key_rows, "seq", axis=0, tiled=True)

    full_out, full_stored = layer_forward(values_in, full_weights, seq_index, fetch_full)
    full_low = full_out.astype(jnp.bfloat16)
    tail_rows = shifted(full_low[row_count - 2 :], "seq", 1)
    grouped = jnp.concatenate([tail_rows, full_low[: row_count - 2]], axis=0).reshape(
        row_count // 3, 3 * model_width
    )
    pooled = jnp.dot(grouped, w_pool, preferred_element_type=jnp.float32) + b_pool.astype(
        jnp.float32
    )
    short_out, short_stored = layer_forward(pooled, short_weights, seq_index, fetch_short)
    short_low = short_out.astype(jnp.bfloat16)
    up_rows = jnp.dot(short_low, w_up, preferred_element_type=jnp.float32) + b_up.astype(
        jnp.float32
    )
    block_out = (full_out + up_rows.reshape(row_count, model_width)).astype(jnp.bfloat16)
    out_rows = out_grad[0].astype(jnp.float32) * start_flags[0].astype(jnp.float32)[:, None]
    up_grad = out_rows.reshape(row_count // 3, 3 * model_width).astype(jnp.bfloat16)
    up_weight_grad = jnp.einsum("pd,pe->de", short_low, up_grad, preferred_element_type=jnp.float32)
    up_bias_grad = jnp.sum(up_grad.astype(jnp.float32), axis=0)
    short_grad = jnp.einsum("pe,de->pd", up_grad, w_up, preferred_element_type=jnp.float32)

    def send_short(grad_keys):
        return lax.psum_scatter(
            grad_keys.astype(jnp.bfloat16), "seq", scatter_dimension=0, tiled=True
        ).astype(jnp.float32)

    pooled_grad, short_grads = layer_backward(
        pooled, short_weights, short_stored, short_grad, seq_index, keep_keys, send_short
    )
    pooled_low = pooled_grad.astype(jnp.bfloat16)
    pool_weight_grad = jnp.einsum(
        "pe,pd->ed", grouped, pooled_low, preferred_element_type=jnp.float32
    )
    pool_bias_grad = jnp.sum(pooled_low.astype(jnp.float32), axis=0)
    grouped_grad = jnp.einsum(
        "pd,ed->pe", pooled_low, w_pool, preferred_element_type=jnp.float32
    ).reshape(row_count, model_width)
    carried = shifted(grouped_grad[:2], "seq", -1)
    full_grad = out_rows + jnp.concatenate([grouped_grad[2:], carried], axis=0)
    short_parts = layer_parts(short_grads) + (
        pool_weight_grad,
        pool_bias_grad,
        up_weight_grad,
        up_bias_grad,
    )

    def send_full(grad_keys):
        return lax.psum_scatter(
            grad_keys.astype(jnp.bfloat16), "seq", scatter_dimension=0, tiled=True
        ).astype(jnp.float32)

    input_grad, full_grads = layer_backward(
        values_in, full_weights, full_stored, full_grad, seq_index, keep_keys, send_full
    )
    full_parts = layer_parts(full_grads)
    stacked = tuple(
        (jnp.stack([first, second]) for first, second in zip(full_parts, short_parts[:8]))
    ) + tuple(short_parts[8:])
    shards = (
        lax.psum_scatter(
            stacked[0].astype(jnp.bfloat16), "batch", scatter_dimension=2, tiled=True
        ).astype(jnp.float32),
        lax.psum_scatter(
            stacked[1].astype(jnp.bfloat16), "batch", scatter_dimension=2, tiled=True
        ).astype(jnp.float32),
        lax.psum_scatter(
            stacked[2].astype(jnp.bfloat16), "batch", scatter_dimension=2, tiled=True
        ).astype(jnp.float32),
        lax.psum_scatter(
            stacked[3].astype(jnp.bfloat16), "batch", scatter_dimension=2, tiled=True
        ).astype(jnp.float32),
        lax.psum_scatter(
            stacked[4].astype(jnp.bfloat16), "batch", scatter_dimension=2, tiled=True
        ).astype(jnp.float32),
        lax.psum_scatter(
            stacked[5].astype(jnp.bfloat16), "batch", scatter_dimension=1, tiled=True
        ).astype(jnp.float32),
        lax.psum_scatter(
            stacked[6].astype(jnp.bfloat16), "batch", scatter_dimension=2, tiled=True
        ).astype(jnp.float32),
        lax.psum_scatter(
            stacked[7].astype(jnp.bfloat16), "batch", scatter_dimension=1, tiled=True
        ).astype(jnp.float32),
        lax.psum_scatter(
            stacked[8].astype(jnp.bfloat16), "batch", scatter_dimension=1, tiled=True
        ).astype(jnp.float32),
        lax.psum_scatter(
            stacked[9].astype(jnp.bfloat16), "batch", scatter_dimension=0, tiled=True
        ).astype(jnp.float32),
        lax.psum_scatter(
            stacked[10].astype(jnp.bfloat16), "batch", scatter_dimension=1, tiled=True
        ).astype(jnp.float32),
        lax.psum_scatter(
            stacked[11].astype(jnp.bfloat16), "batch", scatter_dimension=0, tiled=True
        ).astype(jnp.float32),
    )
    merged = jax.tree.map(
        lambda part: part.astype(jnp.float32), lax.psum(for_sending(shards), "seq")
    )
    slope_total = lax.psum(jnp.stack([full_grads[4], short_grads[4]]), ("seq", "batch"))
    return (
        block_out[None],
        input_grad[None],
        merged[0],
        merged[1],
        merged[2],
        merged[3],
        slope_total,
        merged[4],
        merged[5],
        merged[6],
        merged[7],
        merged[8],
        merged[9],
        merged[10],
        merged[11],
    )


def solution(mesh):
    in_specs = (
        P("batch", "seq", None),
        P("batch", "seq", None),
        P("batch", "seq"),
        P(),
        P(),
        P(),
        P(),
        P(),
        P(),
        P(),
        P(),
        P(),
        P(),
        P(),
        P(),
        P(),
    )
    out_specs = (
        P("batch", "seq", None),
        P("batch", "seq", None),
        P(None, None, "batch"),
        P(None, None, "batch"),
        P(None, None, "batch"),
        P(None, None, "batch"),
        P(),
        P(None, None, "batch"),
        P(None, "batch"),
        P(None, None, "batch"),
        P(None, "batch"),
        P(None, "batch"),
        P("batch"),
        P(None, "batch"),
        P("batch"),
    )
    return jax.shard_map(local, mesh=mesh, in_specs=in_specs, out_specs=out_specs, check_vma=False)
```

profile of v0, /device:TPU:0, one launch (start us, length us, event | category | flops | bytes accessed | tf_op | source)
XLA Modules:
  0.0 900.5 jit_solution(12579477619841431051)
XLA Ops:
  18.7 44.0 %all-gather.3.cloned.1.call-done = bf16[1536,1024]{1,0:T(8,128)(2,1)} async-done(((bf16[384,1024]{1,0:T(8,128)(2,1)}), bf16[1536,1024]{1,0:T(8,128)(2,1)}) %all-gather.3.cloned.1.call-update) | async-done | bytes 3145744 | tf_op jit(solution)/shard_map/all_gather | solution.py:293
  62.7 4.7 copy.86
  67.4 4.4 while.72
  72.8 6.5 while.73
  75.0 4.3 fusion.321
  88.0 14.3 %collective-permute-start = (bf16[2,512]{1,0:T(2,128)(2,1)S(1)}, bf16[2,512]{1,0:T(2,128)(2,1)S(1)}, u32[]{:S(2)}, u32[]{:S(2)}) collective-permute-start(bf16[2,512]{1,0:T(2,128)(2,1)S(1)} %slice.186), channel_id=1, source_target_pairs={{0,8},{8,16},{16,24},{1,9},{9,17},{17,25},{2,10},{10,18},{18,26},{... | collective-permute-start | bytes 6152 | tf_op jit(solution)/shard_map/ppermute | solution.py:13
  117.1 42.0 %all-gather.5.cloned.1.call-done = bf16[512,1024]{1,0:T(8,128)(2,1)} async-done(((bf16[128,1024]{1,0:T(8,128)(2,1)}), bf16[512,1024]{1,0:T(8,128)(2,1)}) %all-gather.5.cloned.1.call-update) | async-done | bytes 1048592 | tf_op jit(solution)/shard_map/all_gather | solution.py:296
  163.3 3.8 while.75
  180.4 4.4 while.76
  190.0 56.0 %reduce-scatter.28.cloned.1.call-done = bf16[128,1024]{1,0:T(8,128)(2,1)} async-done(((bf16[512,1024]{1,0:T(8,128)(2,1)}), bf16[128,1024]{1,0:T(8,128)(2,1)}) %reduce-scatter.28.cloned.1.call-update) | async-done | bytes 262160
  256.2 3.8 collective-permute-done.1
  260.0 6.0 fusion.218
  273.9 3.5 broadcast_in_dim.154
  277.4 11.3 %while.77 = (s32[]{:T(128)}, f32[384,8,64]{0,2,1:T(8,128)S(1)}, f32[1536,1024]{0,1:T(8,128)}, f32[8]{0:T(128)S(1)}, s32[]{:T(128)}, /*index=5*/bf16[1536,1024]{0...) while((s32[]{:T(128)}, f32[384,8,64]{0,2,1:T(8,128)S(1)}, ...), condition=%wide.region_32.33_spmd, body=%wide.region_30.32_spmd.sunk | while | flops 776946432 | bytes 37352960 | solution.py:142
  285.8 2.9 fusion.358
  288.7 4.8 convert_element_type.398
  293.5 4.7 copy.129
  310.0 11.5 %copy.98 = bf16[2,2048,512]{1,0,2:T(2,128)(2,1)} copy(bf16[2,2048,512]{2,1,0:T(8,128)(2,1)} %pad_maximum_fusion.1) | data formatting | bytes 8388608 | tf_op jit(solution)/shard_map/stack | solution.py:354
  324.1 3.7 copy.97
  328.5 46.5 %reduce-scatter.30.cloned.1.call-done = bf16[384,1024]{1,0:T(8,128)(2,1)} async-done(((bf16[1536,1024]{1,0:T(8,128)(2,1)}), bf16[384,1024]{1,0:T(8,128)(2,1)}) %reduce-scatter.30.cloned.1.call-update) | async-done | bytes 786448
  381.0 8.7 copy.96
  395.0 3.0 convolution_convert_fusion.3
  425.0 141.1 %all-reduce.12.cloned.1.call-done = (bf16[2,512,1536]{1,0,2:T(2,128)(2,1)}, bf16[2,512,512]{1,0,2:T(2,128)(2,1)}, bf16[2,2048,512]{1,0,2:T(2,128)(2,1)}) async-done(((bf16[2,512,1536]{1,0,2:T(2,128)(2,1)}, bf16[2,512,512]{1,0,2:T(2,128)(2,1)}, bf16[2,2048,512]{1,0,2:T(2,128)(2,1)}), (bf16[2,512,1536]{1,0,2:T(2,128)(2,1)}, bf16[2,512,512]{1,0,2:T(2,128)(2,1)}, ...) | async-done | bytes 8388624
  572.0 30.8 %reduce-scatter.26.cloned.1.call-done = bf16[512,192]{0,1:T(8,128)(2,1)} async-done(((bf16[512,1536]{0,1:T(8,128)(2,1)}), bf16[512,192]{0,1:T(8,128)(2,1)}) %reduce-scatter.26.cloned.1.call-update) | async-done | bytes 196624 | tf_op jit(solution)/shard_map/reduce_scatter | solution.py:387
  602.9 34.2 %reduce-scatter.24.cloned.1.call-done = bf16[1536,64]{0,1:T(8,128)(2,1)} async-done(((bf16[1536,512]{0,1:T(8,128)(2,1)}), bf16[1536,64]{0,1:T(8,128)(2,1)}) %reduce-scatter.24.cloned.1.call-update) | async-done | bytes 196624 | tf_op jit(solution)/shard_map/reduce_scatter | solution.py:381
  637.0 50.9 %reduce-scatter.22.cloned.1.call-done = bf16[2,512,256]{2,1,0:T(8,128)(2,1)} async-done(((bf16[2,512,2048]{2,1,0:T(8,128)(2,1)}), bf16[2,512,256]{2,1,0:T(8,128)(2,1)}) %reduce-scatter.22.cloned.1.call-update) | async-done | bytes 524304 | tf_op jit(solution)/shard_map/reduce_scatter | solution.py:369
  697.6 14.1 %all-reduce.5 = (bf16[512]{0:T(512)(128)(2,1)S(1)}, bf16[1536]{0:T(1024)(128)(2,1)S(1)}) all-reduce(bf16[512]{0:T(512)(128)(2,1)} %get-tuple-element.686, bf16[1536]{0:T(1024)(128)(2,1)S(1)} %copy-done.78), channel_id=13, replica_groups=mesh['seq'=4,'batch'=8] {'batch'}, use_global_device_ids=true, to_apply=%region_68.69.clone | all-reduce | flops 2048 | bytes 8192
  712.5 38.2 %psum.95 = f32[2,8]{1,0:T(2,128)} all-reduce(f32[2,8]{1,0:T(2,128)S(1)} %pad_maximum_fusion.15), channel_id=1, replica_groups=mesh['seq'=4,'batch'=8] {'seq','batch'}, use_global_device_ids=true, to_apply=%region_52.53 | all-reduce | flops 16 | bytes 128 | tf_op jit(solution)/shard_map/psum | solution.py:397
  755.4 25.8 %reduce-scatter.32.cloned.1.call-done = bf16[64,4]{1,0:T(8,128)(2,1)} async-done(((bf16[512,4]{1,0:T(8,128)(2,1)}), bf16[64,4]{1,0:T(8,128)(2,1)}) %reduce-scatter.32.cloned.1.call-update) | async-done | bytes 528
  782.1 29.5 %reduce-scatter.34.cloned.1.call-done = bf16[64,4]{1,0:T(8,128)(2,1)} async-done(((bf16[512,4]{1,0:T(8,128)(2,1)}), bf16[64,4]{1,0:T(8,128)(2,1)}) %reduce-scatter.34.cloned.1.call-update) | async-done | bytes 528
  812.4 10.1 %all-reduce.7 = (bf16[2,2,64]{2,1,0:T(2,128)(2,1)S(1)}, bf16[2,2,64]{2,1,0:T(2,128)(2,1)S(1)}, bf16[2,256]{1,0:T(2,128)(2,1)S(1)}, bf16[2,64]{1,0:T(2,128)(2,1)S...) all-reduce(bf16[2,2,64]{2,1,0:T(2,128)(2,1)S(1)} %copy.132, ...), channel_id=1, replica_groups=mesh['seq'=4,'batch'=8] {'seq'}, use_global_device_ids=true, to_apply=%region_41.42 | all-reduce | flops 1408 | bytes 5632 | tf_op jit(solution)/shard_map/psum | solution.py:395
  826.0 57.2 %all-reduce.14.cloned.1.call-done = (bf16[2,512,192]{1,0,2:T(2,128)(2,1)}, bf16[2,512,64]{1,0,2:T(2,128)(2,1)}, bf16[2,2048,64]{1,0,2:T(2,128)(2,1)}, bf16[2,512...) async-done(((bf16[2,512,192]{1,0,2:T(2,128)(2,1)}, bf16[2,512,64]{1,0,2:T(2,128)(2,1)}, bf16[2,2048,64]{1,0,2:T(2,128)(2,1)}, ...) | async-done | bytes 1966096 | tf_op jit(solution)/shard_map/psum | solution.py:395
  (480 shorter events, 188.1 us)
Async XLA Ops:
  7.2 107.8 %copy-start = (bf16[512,1536]{1,0:T(8,128)(2,1)S(1)}, bf16[512,1536]{1,0:T(8,128)(2,1)}, u32[]{:S(2)}) copy-start(bf16[512,1536]{1,0:T(8,128)(2,1)} %param.42) | copy-start | bytes 4718596
  7.2 55.5 %all-gather.3.cloned.1.call-start = ((), (), s32[]{:S(2)}) async-start(), calls=%async_computation.9 | async-start | bytes 3932160 | tf_op jit(solution)/shard_map/all_gather | solution.py:293
  11.8 94.5 %copy-start.73 = (f32[1,1,512]{2,1,0:T(1,128)}, f32[1,1,512]{2,1,0:T(1,128)S(1)}, u32[]{:S(2)}) copy-start(f32[1,1,512]{2,1,0:T(1,128)S(1)} %get-tuple-element.727) | copy-start | bytes 6148
  15.9 143.2 %all-gather.5.cloned.1.call-start = ((), (), s32[]{:S(2)}) async-start(), calls=%async_computation.10 | async-start | bytes 1310720 | tf_op jit(solution)/shard_map/all_gather | solution.py:296
  88.0 15.6 %collective-permute-start = (bf16[2,512]{1,0:T(2,128)(2,1)S(1)}, bf16[2,512]{1,0:T(2,128)(2,1)S(1)}, u32[]{:S(2)}, u32[]{:S(2)}) collective-permute-start(bf16[2,512]{1,0:T(2,128)(2,1)S(1)} %slice.186), channel_id=1, source_target_pairs={{0,8},{8,16},{16,24},{1,9},{9,17},{17,25},{2,10},{10,18},{18,26},{... | collective-permute-start | bytes 6152 | tf_op jit(solution)/shard_map/ppermute | solution.py:13
  106.0 62.2 %copy-start.12 = (f32[128,512]{1,0:T(8,128)}, f32[128,512]{1,0:T(8,128)S(1)}, u32[]{:S(2)}) copy-start(f32[128,512]{1,0:T(8,128)S(1)} %get-tuple-element.747) | copy-start | bytes 786436
  109.6 136.4 %reduce-scatter.28.cloned.1.call-start = ((), (), s32[]{:S(2)}) async-start(), calls=%async_computation.14 | async-start | bytes 1310720
  184.8 62.4 %copy-start.13 = (f32[128,512]{1,0:T(8,128)S(1)}, f32[128,512]{1,0:T(8,128)}, u32[]{:S(2)}) copy-start(f32[128,512]{1,0:T(8,128)} %copy-done.12) | copy-start | bytes 786436
  184.8 62.4 %copy-start.74 = (f32[1,1,512]{2,1,0:T(1,128)S(1)}, f32[1,1,512]{2,1,0:T(1,128)}, u32[]{:S(2)}) copy-start(f32[1,1,512]{2,1,0:T(1,128)} %copy-done.73) | copy-start | bytes 6148
  184.8 62.4 %copy-start.92 = (f32[128]{0:T(128)S(1)}, f32[128]{0:T(128)}, u32[]{:S(2)}) copy-start(f32[128]{0:T(128)} %copy-done.91) | copy-start | bytes 1540
  184.8 62.4 %copy-start.101 = (f32[128]{0:T(128)S(1)}, f32[128]{0:T(128)}, u32[]{:S(2)}) copy-start(f32[128]{0:T(128)} %copy-done.100) | copy-start | bytes 1540
  189.8 60.2 %copy-start.105 = (f32[128]{0:T(128)S(1)}, f32[128]{0:T(128)}, u32[]{:S(2)}) copy-start(f32[128]{0:T(128)} %copy-done.104) | copy-start | bytes 1540
  189.8 60.5 %copy-start.26 = (f32[128,512]{1,0:T(8,128)S(1)}, f32[128,512]{1,0:T(8,128)}, u32[]{:S(2)}) copy-start(f32[128,512]{1,0:T(8,128)} %copy-done.25) | copy-start | bytes 786436
  189.9 185.2 %reduce-scatter.30.cloned.1.call-start = ((), (), s32[]{:S(2)}) async-start(), calls=%async_computation.15 | async-start | bytes 3932160
  189.9 61.1 %copy-start.45 = (bf16[128,8,64]{0,2,1:T(8,128)(2,1)}, bf16[128,8,64]{0,2,1:T(8,128)(2,1)S(1)}, u32[]{:S(2)}) copy-start(bf16[128,8,64]{0,2,1:T(8,128)(2,1)S(1)} %multiply_convert_fusion.4) | copy-start | bytes 393220
  254.5 5.5 collective-permute-start.1
  298.2 267.9 %all-reduce.12.cloned.1.call-start = ((), (), s32[]{:S(2)}) async-start(), calls=%async_computation.20 | async-start | bytes 16777216
  321.9 54.7 %copy-start.2 = (bf16[1,384,512]{2,1,0:T(8,128)(2,1)S(1)}, bf16[1,384,512]{2,1,0:T(8,128)(2,1)}, u32[]{:S(2)}) copy-start(bf16[1,384,512]{2,1,0:T(8,128)(2,1)} %param.28) | copy-start | bytes 1179652
  321.9 54.7 %copy-start.50 = (f32[384]{0:T(512)S(1)}, f32[384]{0:T(512)}, u32[]{:S(2)}) copy-start(f32[384]{0:T(512)} %copy-done.49) | copy-start | bytes 4612
  321.9 54.7 %copy-start.62 = (f32[384]{0:T(512)S(1)}, f32[384]{0:T(512)}, u32[]{:S(2)}) copy-start(f32[384]{0:T(512)} %copy-done.61) | copy-start | bytes 4612
  389.7 213.1 %reduce-scatter.26.cloned.1.call-start = ((), (), s32[]{:S(2)}) async-start(), calls=%async_computation.13 | async-start | bytes 1769472 | tf_op jit(solution)/shard_map/reduce_scatter | solution.py:387
  394.9 242.1 %reduce-scatter.24.cloned.1.call-start = ((), (), s32[]{:S(2)}) async-start(), calls=%async_computation.12 | async-start | bytes 1769472 | tf_op jit(solution)/shard_map/reduce_scatter | solution.py:381
  398.0 289.9 %reduce-scatter.22.cloned.1.call-start = ((), (), s32[]{:S(2)}) async-start(), calls=%async_computation.11 | async-start | bytes 4718592 | tf_op jit(solution)/shard_map/reduce_scatter | solution.py:369
  405.3 345.3 %reduce-scatter.38.cloned.1.call-start = ((), (), s32[]{:S(2)}) async-start(), calls=%async_computation.19 | async-start | bytes 147456
  415.1 336.3 %reduce-scatter.36.cloned.1.call-start = ((), (), s32[]{:S(2)}) async-start(), calls=%async_computation.18 | async-start | bytes 589824
  417.7 363.5 %reduce-scatter.32.cloned.1.call-start = ((), (), s32[]{:S(2)}) async-start(), calls=%async_computation.16 | async-start | bytes 147456
  422.7 265.2 %copy-start.21 = (bf16[1,384,512]{2,1,0:T(8,128)(2,1)S(1)}, bf16[1,384,512]{2,1,0:T(8,128)(2,1)}, u32[]{:S(2)}) copy-start(bf16[1,384,512]{2,1,0:T(8,128)(2,1)} %param.29) | copy-start | bytes 1179652
  423.8 387.7 %reduce-scatter.34.cloned.1.call-start = ((), (), s32[]{:S(2)}) async-start(), calls=%async_computation.17 | async-start | bytes 147456
  423.9 265.4 %copy-start.95 = (bf16[1536]{0:T(1024)(128)(2,1)S(1)}, bf16[1536]{0:T(1024)(128)(2,1)}, u32[]{:S(2)}) copy-start(bf16[1536]{0:T(1024)(128)(2,1)} %param.43) | copy-start | bytes 9220
  425.0 458.2 %all-reduce.14.cloned.1.call-start = ((), (), s32[]{:S(2)}) async-start(), calls=%async_computation.21 | async-start | bytes 3932160 | tf_op jit(solution)/shard_map/psum | solution.py:395
  568.2 122.6 %copy-start.58 = (f32[128,3]{0,1:T(4,128)S(1)}, f32[128,3]{0,1:T(4,128)}, u32[]{:S(2)}) copy-start(f32[128,3]{0,1:T(4,128)} %copy-done.57) | copy-start | bytes 4612
  691.7 61.4 %copy-start.60 = (f32[384]{0:T(512)S(1)}, f32[384]{0:T(512)}, u32[]{:S(2)}) copy-start(f32[384]{0:T(512)} %copy-done.59) | copy-start | bytes 4612
  (98 other events, 457.7 us)
Sparse Core Ops, SparseCore 0:
  16.0 46.6 all-gather.2
  109.7 49.3 all-gather.4
  190.0 55.9 reduce-scatter.27
  298.4 76.6 reduce-scatter.29
  389.8 176.2 all-reduce.11
  568.4 34.3 reduce-scatter.25
  605.3 31.7 reduce-scatter.23
  639.4 48.4 reduce-scatter.21
  690.3 28.3 reduce-scatter.37
  720.8 29.2 reduce-scatter.35
  753.0 28.0 reduce-scatter.31
  783.2 28.2 reduce-scatter.33
  816.4 66.7 all-reduce.13
where the time goes:
time: 912 us; the launch traced here: 900 us
  waiting for transfers between devices  563 us (62%)
  local copies, waits for them, and re-layouts  101 us (11%)
  matrix products  80.5 us (9%)
  blocking collectives  62.4 us (7%)
  other arithmetic  58.2 us (6%)
  starting transfers between devices  17.3 us (2%)
  between operations  17.2 us (2%)
    unnamed x20, waiting for transfers between devices  299 us
    psum x1, waiting for transfers between devices, local(): lax.psum(for_sending(shards), 'seq')  57.2 us
    reduce_scatter x1, waiting for transfers between devices, local(): lax.psum_scatter(stacked[4].astype(jnp.bfloat16), 'batch', scatter_dimens...  50.9 us
    all_gather x1, waiting for transfers between devices, fetch_full(): return lax.all_gather(key_rows, 'seq', axis=0, tiled=True)  44 us
    all_gather x1, waiting for transfers between devices, fetch_short(): return lax.all_gather(key_rows, 'seq', axis=0, tiled=True)  42 us
    psum x1, blocking collectives, local(): lax.psum(jnp.stack([full_grads[4], short_grads[4]]), ('seq', 'batch'))  38.2 us
    unnamed x247, local copies, waits for them, and re-layouts  36.9 us
    reduce_scatter x1, waiting for transfers between devices, local(): lax.psum_scatter(stacked[8].astype(jnp.bfloat16), 'batch', scatter_dimens...  34.2 us
  transfers between devices with their start and end apart: 15, of which 13 were waited for; matrix products, arithmetic and copies ran while one was open for 11% of the time, Pallas kernels for 0%

commit v1 on v0

v1 whole, which is shorter than its diff:
```python
import jax
import jax.numpy as jnp
from jax import lax
from jax.experimental import pallas as pl
from jax.experimental.pallas import tpu as pltpu
from jax.sharding import PartitionSpec as P

EPSILON = 1e-05
NEGATIVE = -1e30
HEAD = 64
SCALE = HEAD ** (-0.5)
POS = 128
BQ = 256
F32 = jnp.float32
BF = jnp.bfloat16
VMEM_LIMIT = 60 * 1024 * 1024
GELU_A = 0.7978845608028654
GELU_B = 0.044715


def dims(a, b, ca, cb):
    return lax.dot_general(a, b, (((ca,), (cb,)), ((), ())), preferred_element_type=F32)


def mm(a, b):
    return dims(a, b, 1, 0)


def nt(a, b):
    return dims(a, b, 1, 1)


def tn(a, b):
    return dims(a, b, 0, 0)


def flip(a):
    return jnp.transpose(a)


def iota(shape, axis):
    return lax.broadcasted_iota(jnp.int32, shape, axis)


def standard(x):
    centred = x - jnp.mean(x, axis=-1, keepdims=True)
    rstd = lax.rsqrt(jnp.mean(centred * centred, axis=-1, keepdims=True) + EPSILON)
    return centred * rstd, rstd


TILE = 64


def tiles(rows, size):
    return [slice(at, min(at + size, rows)) for at in range(0, rows, size)]


def norm_into(source, gain, bias, target, first=0):
    rows = source.rows
    for tile in tiles(rows, TILE):
        target[pl.ds(first + tile.start, tile.stop - tile.start), :] = (
            standard(source(tile))[0] * gain + bias
        ).astype(BF)


class Rows:
    def __init__(self, rows, read):
        self.rows, self.read = rows, read

    def __call__(self, tile):
        return self.read(tile)


def norm_back(x, gain, grad, put, rows):
    gain_sum = bias_sum = None
    for tile in tiles(rows, TILE):
        xhat, rstd = standard(x(tile))
        given = grad(tile)
        inner = given * gain
        put(
            tile,
            rstd
            * (
                inner
                - jnp.mean(inner, axis=-1, keepdims=True)
                - xhat * jnp.mean(inner * xhat, axis=-1, keepdims=True)
            ),
        )
        one = jnp.sum(given * xhat, axis=0, keepdims=True)
        two = jnp.sum(given, axis=0, keepdims=True)
        gain_sum = one if gain_sum is None else gain_sum + one
        bias_sum = two if bias_sum is None else bias_sum + two
    return gain_sum, bias_sum


def ffn_forward(normal, w_in, b_in, act, rate, rows, ff):
    for lanes in tiles(ff, 256):
        for tile in tiles(rows, 128):
            value, slope = gelu_both(mm(normal[tile, :], w_in[:, lanes]) + b_in[0:1, lanes])
            act[tile, lanes] = value.astype(BF)
            rate[tile, lanes] = slope.astype(BF)


def ffn_backward(branch, w_back, rate, dpre, sums, rows, ff):
    for lanes in tiles(ff, 512):
        value = (nt(branch[...], w_back[lanes, :]) * rate[:, lanes].astype(F32)).astype(BF)
        dpre[:, lanes] = value
        sums[:, lanes] = jnp.sum(value.astype(F32), axis=0, keepdims=True)


def gelu_both(x):
    square = x * x
    half = 0.5 * jnp.tanh(x * (GELU_A + GELU_A * GELU_B * square)) + 0.5
    value = x * half
    return value, half + (value - value * half) * (2.0 * GELU_A + 6.0 * GELU_A * GELU_B * square)


def rows_at(start, size):
    return pl.ds(pl.multiple_of(start, 16), size)


def lone(value, lane):
    return jnp.where(iota((1, 128), 1) == lane, value, 0.0)


def spread(target, first, value):
    for l in range(target.shape[0]):
        target[l, pl.ds(first, value.shape[0], stride=3), :] = value[:, l * 128 : (l + 1) * 128]


def lanes_at(ref, start, width):
    if width % 128 == 0:
        return ref[:, pl.ds(pl.multiple_of(start, 128), width)]
    total = ref.shape[1]
    pick = (iota((total, width), 0) == iota((total, width), 1) + start).astype(F32).astype(BF)
    return mm(ref[...], pick).astype(BF)


def place_positions(kaug, width):
    length = kaug.shape[0]
    row = iota((length, POS), 0)
    lane = iota((length, POS), 1)
    value = jnp.where(lane < 3, (row >> 7) << 7, jnp.where(lane < 6, row & 127, 0))
    kaug[:, width : width + POS] = value.astype(F32).astype(BF)


def slope_rows(slope, length):
    full = jnp.full((POS, length), slope, F32)
    first = full.astype(BF)
    rest = full - first.astype(F32)
    second = rest.astype(BF)
    third = (rest - second.astype(F32)).astype(BF)
    row = iota((POS, length), 0)
    part = jnp.where(
        (row == 0) | (row == 3),
        first.astype(F32),
        jnp.where(
            (row == 1) | (row == 4),
            second.astype(F32),
            jnp.where((row == 2) | (row == 5), third.astype(F32), 0.0),
        ),
    )
    return part.astype(BF)


def prepare(q, k, slopes, kaug, qa):
    length, width = q.shape
    kaug[:, 0:width] = k
    turned = flip(q) * SCALE
    row = iota((width, length), 0)
    for h, slope in enumerate(slopes):
        own = (row >= HEAD * h) & (row < HEAD * h + HEAD)
        qa[h, 0:width, :] = jnp.where(own, turned, 0.0).astype(BF)
        qa[h, width : width + POS, :] = slope_rows(slope, length)


def causal():
    return iota((BQ, BQ), 0) <= iota((BQ, BQ), 1)


def attend(kaug, qa, vt, mixt, lse, heads):
    length = kaug.shape[0]
    for i in range(length // BQ):
        here = slice(i * BQ, (i + 1) * BQ)
        spans = [slice(j * BQ, (j + 1) * BQ) for j in range(i + 1)]
        for h in range(heads):
            qh = qa[h, :, here]
            scores, top = [], None
            for span in spans:
                score = mm(kaug[span, :], qh)
                if span == here:
                    score = jnp.where(causal(), score, NEGATIVE)
                scores.append(score)
                one = jnp.max(score, axis=0, keepdims=True)
                top = one if top is None else jnp.maximum(top, one)
            own = slice(HEAD * h, HEAD * h + HEAD)
            total = out = None
            for span, score in zip(spans, scores):
                soft = jnp.exp(score - top)
                one = jnp.sum(soft, axis=0, keepdims=True)
                part = mm(vt[own, span], soft.astype(BF))
                total = one if total is None else total + one
                out = part if out is None else out + part
            mixt[own, here] = out / total
            lse[h : h + 1, here] = top + jnp.log(total)


def attend_back(kaug, qa, v, kta, qm, doa, dom, delta, lse, dk, dv, dqt, heads):
    length = kaug.shape[0]
    dk[...] = jnp.zeros_like(dk)
    dv[...] = jnp.zeros_like(dv)
    slope_sums = [jnp.zeros((1, BQ), F32) for _ in range(heads)]
    for i in range(length // BQ):
        off = i * BQ
        here = slice(off, off + BQ)
        for h in range(heads):
            qh = qa[h, :, here]
            doh = doa[h, :, here]
            row_lse = lse[h : h + 1, here]
            row_delta = delta[h : h + 1, here]
            queries = qm[h, here, :]
            grads = dom[h, here, :]
            turned = None
            for part in ((here, True),) + (((slice(0, off), False),) if off else ()):
                span, masked = part
                soft = jnp.exp(mm(kaug[span, :], qh) - row_lse)
                if masked:
                    soft = jnp.where(causal(), soft, 0.0)
                score = (soft * (mm(v[span, :], doh) - row_delta)).astype(BF)
                dv[span, :] += mm(soft.astype(BF), grads)
                dk[span, :] += mm(score, queries)
                more = mm(kta[h, :, span], score)
                turned = more if turned is None else turned + more
            dqt[HEAD * h : HEAD * h + HEAD, here] = turned[0:HEAD, :] * SCALE
            spot = (off + iota((1, BQ), 1)).astype(F32)
            slope_sums[h] = slope_sums[h] + (
                turned[HEAD + 1 : HEAD + 2, :]
                + turned[HEAD + 2 : HEAD + 3, :]
                - spot * turned[HEAD : HEAD + 1, :]
            )
    return slope_sums


def prepare_back(q, k, do, mixt, kta, qm, doa, dom, delta, heads):
    length, width = q.shape
    kt = flip(k)
    dot = flip(do)
    lane = iota((length, width), 1)
    row = iota((width, length), 0)
    extra = iota((16, length), 0)
    column = iota((16, length), 1)
    extras = jnp.where(
        extra == 0,
        1,
        jnp.where(extra == 1, (column >> 7) << 7, jnp.where(extra == 2, column & 127, 0)),
    )
    for h in range(heads):
        own = slice(HEAD * h, HEAD * h + HEAD)
        kta[h, 0:HEAD, :] = kt[own, :].astype(BF)
        kta[h, HEAD : HEAD + 16, :] = extras.astype(F32).astype(BF)
        mine = (lane >= HEAD * h) & (lane < HEAD * h + HEAD)
        qm[h] = jnp.where(mine, q.astype(F32) * SCALE, 0.0).astype(BF)
        dom[h] = jnp.where(mine, do.astype(F32), 0.0).astype(BF)
        doa[h] = jnp.where((row >= HEAD * h) & (row < HEAD * h + HEAD), dot, 0.0).astype(BF)
        delta[h : h + 1, :] = jnp.sum(dot[own, :] * mixt[own, :], axis=0, keepdims=True)


def attend_scratch(length, width, heads, lead=()):
    wide = width + POS
    return [
        pltpu.VMEM(lead + (length, wide), BF),
        pltpu.VMEM(lead + (heads, wide, length), BF),
    ]


def back_scratch(length, width, heads):
    return [
        pltpu.VMEM((heads, HEAD + 16, length), BF),
        pltpu.VMEM((heads, length, width), BF),
        pltpu.VMEM((heads, width, length), BF),
        pltpu.VMEM((heads, length, width), BF),
        pltpu.VMEM((8, length), F32),
        pltpu.VMEM((length, width), F32),
        pltpu.VMEM((length, width), F32),
        pltpu.VMEM((width, length), F32),
    ]


NEAR = "near"
HELD = "held"
ALL = -1
LOAD = -2
FAR = "far"
PART = "part"
HOLD = "hold"
RAW = "raw"


def keeps(n):
    return n <= 4


def hold(n):
    return HOLD if keeps(n) else FAR


def held(n):
    return HELD if keeps(n) else ALL


def smem():
    return pl.BlockSpec(memory_space=pltpu.SMEM)


def vmem():
    return pl.BlockSpec(memory_space=pltpu.VMEM)


def anywhere():
    return pl.BlockSpec(memory_space=pl.ANY)


class Held:
    def __init__(self, source, target, semaphore):
        self.copy = pltpu.make_async_copy(source, target, semaphore)
        self.target = target
        self.waited = False
        self.copy.start()

    def get(self):
        if not self.waited:
            self.copy.wait()
            self.waited = True
        return self.target


class Far:
    def __init__(self, ref, out, semaphores):
        self.ref, self.out, self.semaphores = ref, out, semaphores
        self.copies = []

    def send(self, index=None):
        source = self.ref if index is None else self.ref.at[index]
        target = self.out if index is None else self.out.at[index]
        self.copies.append(pltpu.make_async_copy(source, target, self.semaphores.at[len(self.copies)]))
        self.copies[-1].start()

    def finish(self):
        if not self.copies:
            self.send()
        for copy in self.copies:
            copy.wait()


class Here:
    def __init__(self, ref):
        self.ref = ref

    def get(self):
        return self.ref

    def send(self, index=None):
        pass

    def finish(self):
        pass


def padded(shape, dtype):
    lead = 1
    for extent in shape[:-2]:
        lead *= extent
    tall = shape[-2] if len(shape) > 1 else 1
    return lead * -(-tall // 16) * 16 * -(-shape[-1] // 128) * 128 * jnp.dtype(dtype).itemsize


def in_hbm(array):
    return pltpu.with_memory_space_constraint(array, pltpu.HBM)


def in_vmem(array):
    return pltpu.with_memory_space_constraint(array, pltpu.VMEM)


def call(body, name, ins, specs, outs, scratch=(), after=(), spare=10, weight=10, aliases=None):
    held = [i for i, spec in enumerate(specs) if isinstance(spec, int)]
    shapes = [ins[i].shape[1:] if specs[i] >= 0 else ins[i].shape for i in held]
    kinds = [out[2] if len(out) > 2 else NEAR for out in outs]
    far = [i for i, kind in enumerate(kinds) if kind in (FAR, PART)]
    far_shapes = [out[0] if kind is FAR else out[0][1:] for out, kind in zip(outs, kinds)]
    more = [pltpu.VMEM(shape, ins[i].dtype) for i, shape in zip(held, shapes)]
    more += [pltpu.VMEM(far_shapes[i], outs[i][1]) for i in far]
    if held:
        more.append(pltpu.SemaphoreType.DMA((len(held),)))
    if far:
        more.append(pltpu.SemaphoreType.DMA((len(far), 8)))
    count, own = len(ins), len(scratch)
    used = sum(padded(shape, ins[i].dtype) for i, shape in zip(held, shapes))
    used += sum(padded(shape, out[1]) for shape, out, kind in zip(far_shapes, outs, kinds) if kind is not HOLD)
    used += sum(padded(a.shape, a.dtype) for a, spec in zip(ins, specs) if spec is NEAR)
    used += sum(padded(s.shape, s.dtype) for s in scratch if len(s.shape) > 1 and s.dtype in (F32, BF))
    limit = min(VMEM_LIMIT, int(used * (1.1 if spare >= 10 else 1.0)) + spare * 1024 * 1024)

    def kernel(*refs):
        refs = list(refs)
        operands = refs[:count]
        results = refs[count + len(after) : count + len(after) + len(outs)]
        rest = refs[count + len(after) + len(outs) :]
        temporary, rest = rest[:own], rest[own:]
        targets, rest = rest[: len(held)], rest[len(held) :]
        sources, rest = rest[: len(far)], rest[len(far) :]
        for at, i in enumerate(held):
            source = operands[i] if specs[i] < 0 else operands[i].at[specs[i]]
            operands[i] = Held(source, targets[at], rest[0].at[at])
        for at, i in enumerate(far):
            target = results[i].at[outs[i][3]] if kinds[i] is PART else results[i]
            results[i] = Far(sources[at], target, rest[-1].at[at])
        for i, kind in enumerate(kinds):
            results[i] = Here(results[i]) if kind is HOLD else results[i]
        for i, spec in enumerate(specs):
            operands[i] = Here(operands[i]) if spec is HELD else operands[i]
        body(*operands, *results, *temporary)
        for i in held:
            operands[i].get()
        for i in far:
            results[i].finish()

    pinned = pl.BlockSpec(memory_space=pltpu.HBM)
    spec_of = lambda spec: anywhere() if spec == LOAD else pinned if isinstance(spec, int) or spec is RAW else vmem() if spec in (NEAR, HELD) else spec
    shape_of = {NEAR: jax.ShapeDtypeStruct, HOLD: pltpu.VMEM, FAR: pltpu.HBM, PART: pltpu.HBM}
    place = lambda a, spec: in_hbm(a) if spec is RAW or isinstance(spec, int) and spec != LOAD else in_vmem(a) if spec is HELD else a
    return pl.pallas_call(
        kernel,
        out_shape=[shape_of[kind](out[0], out[1]) for out, kind in zip(outs, kinds)],
        in_specs=[spec_of(spec) for spec in specs] + [anywhere()] * len(after),
        out_specs=[pinned if kind in (FAR, PART) else vmem() for kind in kinds],
        scratch_shapes=list(scratch) + more,
        compiler_params=pltpu.CompilerParams(vmem_limit_bytes=limit),
        cost_estimate=pl.CostEstimate(flops=weight * 1000000000, bytes_accessed=0, transcendentals=0),
        name=name,
        input_output_aliases=aliases or {},
    )(*[place(a, spec) for a, spec in zip(ins, specs)], *after)


def fold(name, targets, after=(), kind=NEAR, weight=10):
    arrays = []
    for _, blocks in targets:
        for block in blocks:
            for array, _, _ in block:
                if not any(array is other for other in arrays):
                    arrays.append(array)
    where = lambda array: [i for i, other in enumerate(arrays) if other is array][0]
    outs, plan = [], []
    for dtype, blocks in targets:
        outs.append(((sum(block[0][2] for block in blocks), blocks[0][0][0].shape[-1]), dtype) + ((kind,) if kind is HOLD else ()))
        plan.append([(block[0][2], [(where(a), first) for a, first, _ in block]) for block in blocks])

    def body(*refs):
        for target, blocks in zip(refs[len(arrays) :], plan):
            target = target.ref if isinstance(target, Here) else target
            at = 0
            for count, block in blocks:
                total = sum(refs[i][first : first + count, :].astype(F32) for i, first in block)
                target[at : at + count, :] = total.astype(target.dtype)
                at += count

    return call(body, name, arrays, [NEAR] * len(arrays), outs, after=after, weight=weight)


def mask_rows(out_grad, flags, after):
    rows, d = out_grad.shape
    third = rows // 3

    def body(grad_ref, flag_ref, given, whole):
        kept = jnp.where(flag_ref[...] != 0, grad_ref[...].astype(F32), 0.0)
        for l in range(d // 128):
            whole[l] = kept[:, l * 128 : (l + 1) * 128]
        for c in range(3):
            for l in range(d // 128):
                part = slice(c * d + l * 128, c * d + (l + 1) * 128)
                given[:, part] = whole[l, pl.ds(c, third, stride=3), :].astype(BF)

    return call(
        body,
        "mask_rows",
        [out_grad, flags],
        [NEAR, NEAR],
        [((third, 3 * d), BF)],
        [pltpu.VMEM((d // 128, rows, 128), F32)],
        after=after,
    )[0]


def pass_on(array, after, weight=10):
    def body(source, target):
        target[...] = source[...]

    return call(body, "pass_on", [array], [NEAR], [(array.shape, array.dtype)], after=after, weight=weight)[0]


def first_rows(pieces, wq, lnp):
    rows, d = pieces[0].shape
    width = wq.shape[1]

    def body(*refs):
        piece_refs, (w_ref, ln_ref, attn, qkv) = refs[: len(pieces)], refs[len(pieces) :]
        for k in range(len(pieces)):
            here = slice(k * rows, (k + 1) * rows)
            norm_into(
                Rows(rows, lambda tile, k=k: piece_refs[k][tile, :].astype(F32)),
                ln_ref[0:1, :],
                ln_ref[4:5, :],
                attn,
                k * rows,
            )
            qkv[here, :] = mm(attn[here, :], w_ref.get()[...]).astype(BF)

    outs = [((len(pieces) * rows, d), BF), ((len(pieces) * rows, width), BF)]
    return call(body, "first_rows", [*pieces, wq, lnp], [NEAR] * len(pieces) + [ALL, NEAR], outs)


def first_attention(idx, slopes, pieces, early, wq, lnp, weights, head_count, dh, after):
    n = len(pieces)
    given = [k for k in range(n) if pieces[k] is not None]
    gone = [k for k in range(n) if pieces[k] is None]
    rows, d = pieces[given[0]].shape
    width = wq.shape[1] // 3
    length = n * rows

    def body(*refs):
        idx_ref, slope_ref = refs[0], refs[1]
        piece_refs = dict(zip(given, refs[2 : 2 + len(given)]))
        early_attn, early_qkv, w_ref, ln_ref = refs[2 + len(given) : 6 + len(given)]
        refs = refs[6 + len(given) :]
        sources, refs = refs[: len(weights)], refs[len(weights) :]
        sends, refs = refs[:n], refs[n:]
        attn, qkv, mixt, lse = refs[:4]
        targets, refs = refs[4 : 4 + len(weights)], refs[4 + len(weights) :]
        kaug, qa, vt, whole = refs[:4]
        s = idx_ref[0]
        loads = [
            pltpu.make_async_copy(source if layer is None else source.at[layer], target.ref, refs[4].at[i])
            for i, (source, target, (_, layer)) in enumerate(zip(sources, targets, weights))
        ]
        for load in loads:
            load.start()
        place_positions(kaug, width)
        gain, bias = ln_ref[0:1, :], ln_ref[4:5, :]
        own_weights = None
        for i, k in enumerate(gone):
            at, here = rows_at((s ^ k) * rows, rows), slice(i * rows, (i + 1) * rows)
            attn.ref[at, :] = early_attn[here, :]
            qkv.ref[at, :] = early_qkv[here, :]
        for k in given:
            first = pl.multiple_of((s ^ k) * rows, TILE)
            norm_into(
                Rows(rows, lambda tile, k=k: piece_refs[k][tile, :].astype(F32)), gain, bias, attn.ref, first
            )
            if own_weights is None:
                own_weights = w_ref.get()
            at = rows_at((s ^ k) * rows, rows)
            qkv.ref[at, :] = mm(attn.ref[at, :], own_weights[...]).astype(BF)
        attn.send()
        qkv.send()
        prepare(
            qkv.ref[:, 0:width],
            qkv.ref[:, width : 2 * width],
            [slope_ref[0, s * head_count + h] for h in range(head_count)],
            kaug,
            qa,
        )
        vt[...] = flip(qkv.ref[:, 2 * width :]).astype(BF)
        if dh < width:
            mixt.ref[...] = jnp.zeros(mixt.ref.shape, F32)
        attend(kaug, qa, vt, mixt.ref, lse.ref, head_count)
        mixt.send()
        lse.send()
        whole[...] = flip(mixt.ref[...].astype(BF))
        for k in range(n):
            sends[k][...] = whole[rows_at((s ^ k) * rows, rows), 0:dh]
        for load in loads:
            load.wait()

    outs = [((rows, dh), BF)] * n + [
        ((length, d), BF, hold(n)),
        ((length, 3 * width), BF, hold(n)),
        ((width, length), F32, hold(n)),
        ((8, length), F32, hold(n)),
    ]
    outs += [(weight.shape[-2:], BF, HOLD) for weight, _ in weights]
    scratch = attend_scratch(length, width, head_count) + [
        pltpu.VMEM((width, length), BF),
        pltpu.VMEM((length, width), BF),
        pltpu.SemaphoreType.DMA((max(len(weights), 1),)),
    ]
    result = call(
        body,
        "first_attention",
        [idx, slopes, *[pieces[k] for k in given], *early, wq, lnp, *[in_hbm(weight) for weight, _ in weights]],
        [smem(), smem()] + [NEAR] * (len(given) + 2) + [ALL, NEAR] + [pl.BlockSpec(memory_space=pltpu.HBM)] * len(weights),
        outs,
        scratch,
        after=after,
    )
    return result[:n], result[n : n + 4], result[n + 4 :]


CARRY = 16


def first_ffn(idx, hid, mixes, lnp, w_out, w_in, b_in, w_back, b_back, w_pool, b_pool, after):
    n = len(mixes)
    rows, d = hid.shape
    dh = mixes[0].shape[1]
    ff = b_in.shape[1]
    third = rows // 3

    def body(*refs):
        idx_ref, hid_ref = refs[0], refs[1]
        mix_refs = refs[2 : 2 + n]
        ln_ref, wo, wi, bi, wb, bb, wp, bp = refs[2 + n : 10 + n]
        full_g, pooled, mid, pack, slope, whole, owners = refs[10 + n :]
        s = idx_ref[0]
        middle = hid_ref.get()[...].astype(F32)
        wo = wo.get()
        for k in range(n):
            middle = middle + mm(mix_refs[k][...], wo[rows_at((s ^ k) * dh, dh), :])
            owners[s ^ k] = mix_refs[k][...]
        for j in range(n):
            pack.ref[0:rows, ff + d + j * dh : ff + d + (j + 1) * dh] = owners[j]
        mid.ref[...] = middle
        mid.send()
        norm_into(
            Rows(rows, lambda tile: mid.ref[tile, :]), ln_ref[1:2, :], ln_ref[5:6, :], pack.ref.at[:, ff : ff + d]
        )
        wi, wb = wi.get(), wb.get()
        ffn_forward(pack.ref.at[:, ff : ff + d], wi, bi, pack.ref, slope.ref, rows, ff)
        slope.send()
        total = mid.ref[...] + bb[0:1, :] + mm(pack.ref[0:rows, 0:ff], wb[...])
        for l in range(d // 128):
            whole[l] = total[:, l * 128 : (l + 1) * 128]
        for c in range(3):
            for l in range(d // 128):
                some = whole[l, pl.ds(c, third, stride=3), :]
                part = slice(c * d + l * 128, c * d + (l + 1) * 128)
                full_g.ref[:, part] = some
                pack.ref[rows:, part] = some.astype(BF)
        pack.send()
        wp = wp.get()
        moved = pltpu.roll(mm(pack.ref[rows:, d : 3 * d], wp[0 : 2 * d, :]), 1, 0)
        own = mm(pack.ref[rows:, 0:d], wp[2 * d :, :]) + bp[0:1, :]
        pooled[0:third, :] = (own + jnp.where(iota((third, d), 0) == 0, 0.0, moved)).astype(BF)
        pooled[third:, :] = moved[0:CARRY, :].astype(BF)

    outs = [
        ((third, 3 * d), F32, hold(n)),
        ((third + CARRY, d), BF),
        ((rows, d), F32, hold(n)),
        ((rows + third, ff + 2 * d), BF, hold(n)),
        ((rows, ff), BF, hold(n)),
    ]
    weight = HELD if keeps(n) else 0
    return call(
        body,
        "first_ffn",
        [idx, hid, *mixes, lnp, w_out, w_in, b_in, w_back, b_back, w_pool, b_pool],
        [smem(), ALL] + [NEAR] * (n + 1) + [weight, weight, NEAR, weight, NEAR, ALL, NEAR],
        outs,
        [pltpu.VMEM((d // 128, rows, 128), F32), pltpu.VMEM((n, rows, dh), BF)],
        after=after,
    )


def short_layout(n, m, d, ff):
    kw = d // n
    spans, at = {}, 0
    for name, rows, blocks in (
        ("qkv", 3 * d // m, 1),
        ("out", d // m, 1),
        ("in", kw, ff // m // kw),
        ("back", d // m, ff // n // kw),
        ("up", 3 * d // m, 1),
    ):
        spans[name] = (at, rows, blocks)
        at += rows * blocks
    return spans, at


def ffn_layout(n, m, d, ff):
    kw = d // n
    spans, at = {}, 0
    for name, rows, blocks in (
        ("out", d // m, 1),
        ("in", kw, ff // m // kw),
        ("back", d // m, ff // n // kw),
    ):
        spans[name] = (at, rows, blocks)
        at += rows * blocks
    return spans, at


def last_layout(n, m, d):
    return 3 * d // m, d // m, 3


def pool_unit(unit, n, d):
    kw = d // n
    early = unit < 2 * n
    return early, jnp.where(early, d + unit * kw, unit * kw - 2 * d)


def short_start(idx, given, w_up, w_back, layered, w_pool, after):
    n = len(given)
    third, d3 = given[0].shape
    d, ff = d3 // 3, w_back.shape[0]
    length = n * third

    def body(*refs):
        idx_ref, given_refs = refs[0], refs[1 : 1 + n]
        wu, wb = refs[1 + n].get(), refs[2 + n].get()
        sources, refs = refs[3 + n : 7 + n], refs[7 + n :]
        u, grad, branch, act_grad = refs[:4]
        targets, arrived = refs[4:8], refs[8]
        s = idx_ref[0]
        loads = []
        later = [
            pltpu.make_async_copy(source.at[1] if i < 3 else source, target.ref, arrived.at[n + i])
            for i, (source, target) in enumerate(zip(sources, targets))
        ]
        for k in range(n):
            place = u.ref.at[rows_at((s ^ k) * third, third), :]
            loads.append(pltpu.make_async_copy(given_refs[k], place, arrived.at[k]))
        for load in loads:
            load.start()
        for load in later:
            load.start()
        for load in loads:
            load.wait()
        grad.ref[...] = nt(u.ref[...], wu[...])
        branch.ref[...] = grad.ref[...].astype(BF)
        for lanes in tiles(ff, 512):
            act_grad.ref[:, lanes] = nt(branch.ref[...], wb[lanes, :]).astype(BF)
        for load in later:
            load.wait()

    outs = [
        ((length, d3), BF, HOLD),
        ((length, d), F32, HOLD),
        ((length, d), BF, HOLD),
        ((length, ff), BF, HOLD),
        *[(weight.shape[1:], BF, HOLD) for weight in layered],
        (w_pool.shape, BF, HOLD),
    ]
    return call(
        body,
        "short_start",
        [idx, *given, w_up, w_back, *layered, w_pool],
        [smem()] + [anywhere()] * n + [HELD, HELD] + [RAW] * 4,
        outs,
        [pltpu.SemaphoreType.DMA((n + 4,))],
        after=after,
        weight=100,
    )


def short_layer(
    idx, slopes, pooled, given, begun, full_g, lnp, w_qkv, w_out, w_in, b_in, w_back, b_back, w_pool, w_up, b_up, m, after
):
    n = len(pooled)
    third = pooled[0].shape[0] - CARRY
    given = [] if begun else given
    d = lnp.shape[1]
    ff = b_in.shape[1]
    rows = 3 * third
    length = n * third
    width = 128
    pairs = d // width
    kw = d // n
    spans, packed_rows = short_layout(n, m, d, ff)
    kept_pairs = pairs if length <= 512 else 1

    def body(*refs):
        idx_ref, slope_ref = refs[0], refs[1]
        pool_refs = refs[2 : 2 + n]
        given_refs, refs = refs[2 + n : 2 + n + len(given)], refs[2 + n + len(given) :]
        begun_refs, refs = refs[: len(begun)], refs[len(begun) :]
        (fg, ln_ref, wq, wo, wi, bi, wb, bb, wp, wu, bu) = refs[:11]
        block_out, full_grad, pair, keep, give, small = refs[11:17]
        (
            pooled_s, carry, attn, qkv, mixed, mixt, lse, kaug, qa, vt, middle_s, ffn_in, act, rate,
            back_s, low_grad, low, dmix, dpl, whole, into, into2, arrived,
            kta, qm, doa, dom, delta, dk, dv, dqt, *own,
        ) = refs[17:]
        if begun:
            u_all, grad_s, branch_s, act_grad = [ref.get() for ref in begun_refs]
        else:
            u_all, grad_s, branch_s = own
        s = idx_ref[0]
        mine = idx_ref[1]
        dpre, dqkv = rate, qkv
        loads = []
        for k in range(len(given)):
            place = u_all.at[rows_at((s ^ k) * third, third), :]
            loads.append(pltpu.make_async_copy(given_refs[k], place, arrived.at[k]))
            loads[-1].start()
        for k in range(n):
            pooled_s[rows_at((s ^ k) * third, third), :] = pool_refs[k][0:third, :].astype(F32)
            carry[s ^ k] = pool_refs[k][third:, :].astype(F32)
        for j in range(1, n):
            pooled_s[j * third : j * third + 1, :] += carry[j - 1, 0:1, :]
        norm_into(Rows(length, lambda tile: pooled_s[tile, :]), ln_ref[2:3, :], ln_ref[6:7, :], attn)
        wq = wq.get()
        for c in range(0, 3 * d, 256):
            qkv[:, c : c + 256] = mm(attn[...], wq[:, c : c + 256]).astype(BF)

        def again(t):
            lane = pl.multiple_of(t * width, 128)
            own = t if kept_pairs > 1 else 0
            place_positions(kaug.at[own], width)
            prepare(
                qkv[:, pl.ds(lane, width)],
                qkv[:, pl.ds(d + lane, width)],
                [slope_ref[1, 2 * t + h] for h in range(2)],
                kaug.at[own],
                qa.at[own],
            )
            return kaug.at[own], qa.at[own]

        def forward(t, _):
            lane = pl.multiple_of(t * width, 128)
            own_kaug, own_qa = again(t)
            vt[...] = flip(qkv[:, pl.ds(2 * d + lane, width)]).astype(BF)
            attend(own_kaug, own_qa, vt, mixt.at[t], lse.at[t], 2)
            mixed[:, pl.ds(lane, width)] = flip(mixt[t].astype(BF))
            return 0

        lax.fori_loop(0, pairs, forward, 0)
        wo = wo.get()
        middle_s[...] = pooled_s[...] + mm(mixed[...], wo[...])
        norm_into(Rows(length, lambda tile: middle_s[tile, :]), ln_ref[3:4, :], ln_ref[7:8, :], ffn_in)
        wi, wb = wi.get(), wb.get()
        ffn_forward(ffn_in, wi, bi, act, rate, length, ff)
        low[...] = (middle_s[...] + bb[0:1, :] + mm(act[...], wb[...])).astype(BF)
        mine_rows = rows_at(s * third, third)
        own = low[mine_rows, :]
        wu, full = wu.get(), fg.get()
        for c in range(3):
            part = slice(c * d, (c + 1) * d)
            up = mm(own, wu[:, part]) + bu[0:1, part]
            spread(whole, c, full[:, part] + up)
        for l in range(d // 128):
            block_out.ref[:, l * 128 : (l + 1) * 128] = whole[l].astype(BF)
        block_out.send()

        small = small.ref
        small[...] = jnp.zeros_like(small)
        for load in loads:
            load.wait()
        u = u_all[...]
        if not begun:
            grad_s[...] = nt(u, wu[...])
            branch_s[...] = grad_s[...].astype(BF)
        small[1:2, 0 : 3 * d] = jnp.sum(u.astype(F32), axis=0, keepdims=True)
        small[3:4, 0:d] = jnp.sum(branch_s[...].astype(F32), axis=0, keepdims=True)
        if begun:
            for lanes in tiles(ff, 512):
                value = (act_grad[:, lanes].astype(F32) * rate[:, lanes].astype(F32)).astype(BF)
                dpre[:, lanes] = value
                small[0:1, lanes] = jnp.sum(value.astype(F32), axis=0, keepdims=True)
        else:
            ffn_backward(branch_s, wb, rate, dpre, small.at[0:1, :], length, ff)
        back_s[...] = nt(dpre[...], wi[...])

        def put_middle(tile, value):
            value = grad_s[tile, :] + value
            grad_s[tile, :] = value
            low_grad[tile, :] = value.astype(BF)

        gain_late, bias_late = norm_back(
            lambda tile: middle_s[tile, :], ln_ref[3:4, :], lambda tile: back_s[tile, :], put_middle, length
        )
        dmix[...] = nt(low_grad[...], wo[...]).astype(BF)

        def backward(t, slope_row):
            lane = pl.multiple_of(t * width, 128)
            prepare_back(
                qkv[:, pl.ds(lane, width)],
                qkv[:, pl.ds(d + lane, width)],
                dmix[:, pl.ds(lane, width)],
                mixt.at[t],
                kta,
                qm,
                doa,
                dom,
                delta,
                2,
            )
            own_kaug, own_qa = (kaug.at[t], qa.at[t]) if kept_pairs > 1 else again(t)
            vt2 = qkv.at[:, pl.ds(2 * d + lane, width)]
            sums = attend_back(
                own_kaug, own_qa, vt2, kta, qm, doa, dom, delta, lse.at[t], dk, dv, dqt, 2
            )
            dqkv[:, pl.ds(lane, width)] = flip(dqt[...].astype(BF))
            dqkv[:, pl.ds(d + lane, width)] = dk[...].astype(BF)
            dqkv[:, pl.ds(2 * d + lane, width)] = dv[...].astype(BF)
            for h in range(2):
                slope_row = slope_row + lone(jnp.sum(sums[h], axis=1, keepdims=True), 2 * t + h)
            return slope_row

        slope_row = lax.fori_loop(0, pairs, backward, jnp.zeros((1, 128), F32))
        small[3:4, d : d + 128] = slope_row
        back_s[...] = nt(dqkv[...], wq[...])

        def put_pooled(tile, value):
            dpl[0, tile, :] = (grad_s[tile, :] + value).astype(BF)

        gain_early, bias_early = norm_back(
            lambda tile: pooled_s[tile, :], ln_ref[2:3, :], lambda tile: back_s[tile, :], put_pooled, length
        )
        wide = dpl[0].astype(F32)
        small[2:3, 0:d] = gain_early
        small[2:3, d : 2 * d] = gain_late
        small[2:3, 2 * d : 3 * d] = bias_early
        small[2:3, 3 * d : 4 * d] = bias_late
        small[1:2, 3 * d : 4 * d] = jnp.sum(wide, axis=0, keepdims=True)
        later = pltpu.roll(wide, length - 1, 0)
        dpl[1] = jnp.where(iota((length, d), 0) == length - 1, 0.0, later).astype(BF)
        here, after = dpl[0, mine_rows, :], dpl[1, mine_rows, :]
        pair.ref[...] = dpl[...]
        wp = wp.get()
        given_own = u_all[mine_rows, :].astype(F32)
        spread(whole, 0, given_own[:, 0:d] + nt(here, wp[2 * d :, :]))
        spread(whole, 1, given_own[:, d : 2 * d] + nt(after, wp[0:d, :]))
        spread(whole, 2, given_own[:, 2 * d :] + nt(after, wp[d : 2 * d, :]))
        for l in range(d // 128):
            full_grad.ref[:, l * 128 : (l + 1) * 128] = whole[l]
        full_grad.send()

        def put(name, block, value):
            at, count, _ = spans[name]
            at += block * count
            into[...] = flip(value.astype(BF))
            for far in range(m // 2):
                for bit, target in ((0, keep), (1, give)):
                    start = (mine ^ (2 * far + bit)) * count
                    target[far, at : at + count, :] = into[rows_at(start, count), :]

        def put_tall(name, value):
            at, count, _ = spans[name]
            into2[...] = flip(value.astype(BF))
            for far in range(m // 2):
                for bit, target in ((0, keep), (1, give)):
                    start = (mine ^ (2 * far + bit)) * count
                    target[far, at : at + count, :] = into2[rows_at(start, count), :]

        put_tall("qkv", tn(lanes_at(attn, s * kw, kw), dqkv[...]))
        put("out", 0, tn(lanes_at(mixed, s * kw, kw), low_grad[...]))
        at, count, blocks = spans["in"]
        grad_in = tn(lanes_at(ffn_in, s * kw, kw), dpre[...]).astype(BF)
        for b in range(m):
            for i in range(blocks):
                first = (b * blocks + i) * kw
                here = slice(at + i * count, at + (i + 1) * count)
                piece = grad_in[:, first : first + kw]

                def store(target, far=(mine ^ b) >> 1, here=here, piece=piece):
                    target[far, here, :] = piece

                pl.when(((mine ^ b) & 1) == 0)(lambda: store(keep))
                pl.when(((mine ^ b) & 1) == 1)(lambda: store(give))
        blocks = spans["back"][2]
        for i in range(blocks):
            put("back", i, tn(lanes_at(act, (s * blocks + i) * kw, kw), branch_s[...]))
        put_tall("up", tn(lanes_at(low, s * kw, kw), u))

    outs = [
        ((rows, d), BF, FAR),
        ((rows, d), F32, hold(n)),
        ((2, length, d), BF, hold(n)),
        ((m // 2, packed_rows, kw), BF),
        ((m // 2, packed_rows, kw), BF),
        ((8, ff), F32, hold(n)),
    ]
    scratch = [
        pltpu.VMEM((length, d), F32),
        pltpu.VMEM((n, CARRY, d), F32),
        pltpu.VMEM((length, d), BF),
        pltpu.VMEM((length, 3 * d), BF),
        pltpu.VMEM((length, d), BF),
        pltpu.VMEM((pairs, width, length), F32),
        pltpu.VMEM((pairs, 8, length), F32),
        *attend_scratch(length, width, 2, (kept_pairs,)),
        pltpu.VMEM((width, length), BF),
        pltpu.VMEM((length, d), F32),
        pltpu.VMEM((length, d), BF),
        pltpu.VMEM((length, ff), BF),
        pltpu.VMEM((length, ff), BF),
        pltpu.VMEM((length, d), F32),
        pltpu.VMEM((length, d), BF),
        pltpu.VMEM((length, d), BF),
        pltpu.VMEM((length, d), BF),
        pltpu.VMEM((2, length, d), BF),
        pltpu.VMEM((d // 128, rows, 128), F32),
        pltpu.VMEM((d, kw), BF),
        pltpu.VMEM((3 * d, kw), BF),
        pltpu.SemaphoreType.DMA((n,)),
        *back_scratch(length, width, 2),
    ]
    if not begun:
        scratch += [
            pltpu.VMEM((length, 3 * d), BF),
            pltpu.VMEM((length, d), F32),
            pltpu.VMEM((length, d), BF),
        ]
    return call(
        body,
        "short_layer",
        [idx, slopes, *pooled, *given, *begun, full_g, lnp, w_qkv, w_out, w_in, b_in, w_back, b_back, w_pool, w_up, b_up],
        [smem(), smem()]
        + [NEAR] * n
        + [anywhere()] * len(given)
        + [HELD] * len(begun)
        + [held(n), NEAR, *[HELD if begun else 1] * 3, NEAR, HELD if begun else 1, NEAR]
        + [HELD if begun else ALL] * 2
        + [NEAR],
        outs,
        scratch,
        after=after,
        spare=4 if keeps(n) else 20,
    )


def core_columns(ref, width, core):
    total = ref.shape[1]
    if width % 128 == 0:
        starts = [pl.multiple_of((2 * z + core) * width, 128) for z in range(total // width // 2)]
        return jnp.concatenate([ref[:, pl.ds(start, width)] for start in starts], axis=1)
    shape = (total, total // 2)
    row, column = iota(shape, 0), iota(shape, 1)
    block = lax.div(column, width)
    pick = row == (2 * block + core) * width + (column - block * width)
    return mm(ref[...], pick.astype(F32).astype(BF)).astype(BF)


def first_ffn_back(idx, full_grad, mid, rate, forward, lnp, w_out, w_in, w_back, fetch, n, m):
    rows, d = mid.shape
    ff = rate.shape[1]
    dh = d // n

    def body(*refs):
        idx_ref, grad_ref, mid_ref, rate_ref, forward_ref, ln_ref, wo, wi, wb = refs[:9]
        sources, refs = refs[9 : 9 + len(fetch)], refs[9 + len(fetch) :]
        sends, refs = refs[:n], refs[n:]
        middle_grad, own, give, small = refs[:4]
        targets, refs = refs[4 : 4 + len(fetch)], refs[4 + len(fetch) :]
        dpre, low_ref, branch_ref, back_s, fetched = refs
        loads = [
            pltpu.make_async_copy(source, target.ref, fetched.at[i])
            for i, (source, target) in enumerate(zip(sources, targets))
        ]
        for load in loads:
            load.start()
        s, core = idx_ref[0], idx_ref[1] & 1
        grad = grad_ref.get()[...]
        branch = grad.astype(BF)
        branch_ref[...] = branch
        sums = small.ref
        sums[...] = jnp.zeros_like(sums)
        sums[5:6, 2 * d : 3 * d] = jnp.sum(branch.astype(F32), axis=0, keepdims=True)
        wb, wi, rates = wb.get(), wi.get(), rate_ref.get()
        ffn_backward(branch_ref, wb, rates, dpre, sums.at[4:5, :], rows, ff)
        back_s[...] = nt(dpre[...], wi[...])
        middles, grads = mid_ref.get(), grad_ref.get()

        def put(tile, value):
            value = grads[tile, :] + value
            middle_grad.ref[tile, :] = value
            low_ref[tile, :] = value.astype(BF)

        gain, bias = norm_back(
            lambda tile: middles[tile, :], ln_ref[1:2, :], lambda tile: back_s[tile, :], put, rows
        )
        sums[5:6, 0:d] = gain
        sums[5:6, d : 2 * d] = bias
        small.send()
        middle_grad.send()
        wo = wo.get()
        for k in range(n):
            sends[k][0:rows, :] = nt(low_ref[...], wo[rows_at((s ^ k) * dh, dh), :]).astype(BF)
        groups = forward_ref.get().at[rows:, 0 : 3 * d]
        third = rows // 3
        for k in range(n):
            for i in range(3):
                _, start = pool_unit(3 * (s ^ k) + i, n, d)
                sends[k][rows + i * third : rows + (i + 1) * third, :] = lanes_at(groups, start, dh)
        for target, bit in ((own, 0), (give, 1)):
            target.ref[0:rows, 0 : ff // 2] = core_columns(dpre, ff // m, core ^ bit)
            target.ref[0:rows, ff // 2 : (ff + d) // 2] = core_columns(branch_ref, d // m, core ^ bit)
            target.ref[0:rows, (ff + d) // 2 :] = core_columns(low_ref, d // m, core ^ bit)
        for load in loads:
            load.wait()

    pack = (rows, ff // 2 + d)
    outs = [((2 * rows, dh), BF)] * n + [
        ((rows, d), F32, hold(n)),
        (pack, BF, hold(n)),
        (pack, BF, hold(n)),
        ((8, ff), F32, hold(n)),
        *[(array.shape, array.dtype, HOLD) for array in fetch],
    ]
    weight = HELD if keeps(n) else 0
    result = call(
        body,
        "first_ffn_back",
        [idx, full_grad, mid, rate, forward, lnp, w_out, w_in, w_back, *fetch],
        [smem()] + [held(n)] * 4 + [NEAR, weight, weight, weight] + [anywhere()] * len(fetch),
        outs,
        [pltpu.VMEM((rows, ff), BF), pltpu.VMEM((rows, d), BF), pltpu.VMEM((rows, d), BF)]
        + [pltpu.VMEM((rows, d), F32), pltpu.SemaphoreType.DMA((max(len(fetch), 1),))],
    )
    return result[:n], result[n:]


def halves(n, count):
    bits = [1 << t for t in range(n.bit_length() - 1)]
    return ((bits, range(0, count // 2)), (bits[::-1], range(count // 2, count)))


def kept_orders(n, bits):
    orders = [list(range(n))]
    for bit in bits:
        orders.append([r for r in orders[-1] if not r & bit])
    return orders


def first_ffn_weights(idx, forward, forward_other, back, back_other, n, m, d, ff, after):
    rows = forward.shape[0] // 4 * 3
    kw = d // n
    far = m // 2
    spans, packed_rows = ffn_layout(n, m, d, ff)
    plan = halves(n, far)

    def body(*refs):
        idx_ref, own_f, other_f, own_b, other_b = refs[:5]
        targets = refs[5:9]
        wide_in, wide_back, wide_out = refs[9:]
        s, mine = idx_ref[0], idx_ref[1]
        per, share, count_out = ff // m, ff // n, d // m
        f, g, b, h = own_f.get(), other_f.get(), own_b.get(), other_b.get()
        cut_in, cut_back = ff // 2, (ff + d) // 2
        turned = [flip(x[0:rows, ff : ff + d]).astype(BF) for x in (f, g)]
        for z in range(far):
            part = slice(z * per, (z + 1) * per)
            wide_in[z] = (mm(turned[0], b[0:rows, part]) + mm(turned[1], h[0:rows, part])).astype(BF)
        turned = [flip(x[0:rows, cut_in:cut_back]).astype(BF) for x in (b, h)]
        for j in range(n):
            part = slice(j * share, (j + 1) * share)
            wide_back[j] = (mm(turned[0], f[0:rows, part]) + mm(turned[1], g[0:rows, part])).astype(BF)
        turned = [flip(x[0:rows, cut_back:]).astype(BF) for x in (b, h)]
        for j in range(n):
            part = slice(ff + d + j * kw, ff + d + (j + 1) * kw)
            wide_out[j] = (mm(turned[0], f[0:rows, part]) + mm(turned[1], g[0:rows, part])).astype(BF)
        for half, (bits, places) in enumerate(plan):
            order = kept_orders(n, bits)[0]
            keeps_, gives = [r for r in order if not r & bits[0]], [r for r in order if r & bits[0]]
            for target, chosen in ((targets[2 * half], keeps_), (targets[2 * half + 1], gives)):
                first = 0
                for r in chosen:
                    j = s ^ r
                    for zr in places:
                        z = (mine >> 1) ^ zr
                        at, count, _ = spans["out"]
                        target[first + at : first + at + count, :] = wide_out[j, rows_at(z * count, count), :]
                        at, count, blocks = spans["in"]
                        for i in range(blocks):
                            target[first + at + i * count : first + at + (i + 1) * count, :] = wide_in[
                                z, rows_at(j * kw, kw), i * kw : (i + 1) * kw
                            ]
                        at, count, blocks = spans["back"]
                        for i in range(blocks):
                            target[first + at + i * count : first + at + (i + 1) * count, :] = wide_back[
                                j, rows_at(z * count, count), i * kw : (i + 1) * kw
                            ]
                        first += packed_rows

    outs = [((n // 2 * (far // 2) * packed_rows, kw), BF)] * 4
    scratch = [
        pltpu.VMEM((far, d, ff // m), BF),
        pltpu.VMEM((n, d // 2, ff // n), BF),
        pltpu.VMEM((n, d // 2, kw), BF),
    ]
    return call(
        body,
        "first_ffn_weights",
        [idx, forward, forward_other, back, back_other],
        [smem(), held(n), HELD if keeps(n) else LOAD, held(n), HELD if keeps(n) else LOAD],
        outs,
        scratch,
        after=after,
    )


SMALL = 16


def small_layout(m, kw, d, ff):
    places, row = {}, 0
    for name, size in (("in0", ff // m), ("in1", ff // m), ("up", 3 * d // m)):
        places[name] = (row, 0, size)
        row += -(-size // kw)
    for one, two in (
        ("gain00", "gain01"),
        ("gain10", "gain11"),
        ("bias00", "bias01"),
        ("bias10", "bias11"),
        ("back0", "back1"),
        ("pool", None),
    ):
        places[one] = (row, 0, d // m)
        if two:
            places[two] = (row, kw // 2, d // m)
        row += 1
    places["slopes"] = (row, 0, 0)
    return places


def first_attention_back(
    idx, slopes, qkv, attn, mixt, lse, grads, wq, lnp, small_short, small_ffn, pooled_grad, head_count, dh, m, after
):
    n = len(grads)
    length, d = attn.shape
    rows = length // n
    third = rows // 3
    width = wq.shape[1] // 3
    kw = d // n
    ff = small_ffn.shape[1]
    heads = slopes.shape[1]

    def body(*refs):
        idx_ref, slope_ref, qkv_ref, attn_ref, mixt_ref, lse_ref = refs[:6]
        grad_refs = refs[6 : 6 + n]
        w_ref, ln_ref, short_ref, ffn_ref, pooled_ref = refs[6 + n : 11 + n]
        refs = refs[11 + n :]
        shares, sends, pool = refs[:n], refs[n : 2 * n], refs[2 * n]
        kaug, qa, do, turned, owners, table, groups, kta, qm, doa, dom, delta, dk, dv, dqt = refs[2 * n + 1 :]
        s = idx_ref[0]
        if dh < width:
            do[...] = jnp.zeros_like(do)
            dqt[...] = jnp.zeros_like(dqt)
        for k in range(n):
            do[rows_at((s ^ k) * rows, rows), 0:dh] = grad_refs[k][0:rows, :]
            for i in range(3):
                here = slice(rows + i * third, rows + (i + 1) * third)
                groups[i, rows_at((s ^ k) * third, third), :] = grad_refs[k][here, :]
        place_positions(kaug, width)
        qkv_ref = qkv_ref.get()
        q, k_ = qkv_ref[:, 0:width], qkv_ref[:, width : 2 * width]
        prepare(q, k_, [slope_ref[0, s * head_count + h] for h in range(head_count)], kaug, qa)
        prepare_back(q, k_, do[...], mixt_ref.get(), kta, qm, doa, dom, delta, head_count)
        sums = attend_back(
            kaug, qa, qkv_ref.at[:, 2 * width :], kta, qm, doa, dom, delta, lse_ref.get(), dk, dv, dqt, head_count
        )
        turned[0:width, :] = dqt[...].astype(BF)
        turned[width : 2 * width, :] = flip(dk[...].astype(BF))
        turned[2 * width :, :] = flip(dv[...].astype(BF))
        do[...] = flip(dqt[...].astype(BF))
        for k in range(n):
            here = rows_at((s ^ k) * rows, rows)
            sends[k][0:rows, :] = do[here, 0:dh]
            sends[k][rows : 2 * rows, :] = dk[here, 0:dh].astype(BF)
            sends[k][2 * rows : 3 * rows, :] = dv[here, 0:dh].astype(BF)
        grad_w = mm(turned[...], attn_ref.get()[...])
        for j in range(n):
            for g in range(3):
                owners[j, g * dh : (g + 1) * dh, :] = grad_w[
                    g * width : g * width + dh, j * kw : (j + 1) * kw
                ].astype(BF)
        w_turned = flip(w_ref.get()[...]).astype(F32)
        gain, bias = ln_ref[0:1, :], ln_ref[4:5, :]
        column = jnp.sum(turned[...].astype(F32), axis=1, keepdims=True)
        bias_grad = jnp.sum(w_turned * column, axis=0, keepdims=True)
        gain_grad = (jnp.sum(w_turned * grad_w, axis=0, keepdims=True) - bias * bias_grad) / gain
        once = jnp.where(s == 0, 1.0, 0.0)
        both = ffn_ref.get()[...] + once * short_ref.get()[...]
        slope_row = jnp.zeros((1, 128), F32)
        for h in range(head_count):
            slope_row = slope_row + lone(jnp.sum(sums[h], axis=1, keepdims=True), s * head_count + h)
        table[...] = jnp.zeros_like(table)
        vectors = {
            "in0": both[4:5, :],
            "in1": both[0:1, :],
            "up": both[1:2, 0 : 3 * d],
            "gain00": gain_grad,
            "gain01": both[5:6, 0:d],
            "gain10": both[2:3, 0:d],
            "gain11": both[2:3, d : 2 * d],
            "bias00": bias_grad,
            "bias01": both[5:6, d : 2 * d],
            "bias10": both[2:3, 2 * d : 3 * d],
            "bias11": both[2:3, 3 * d : 4 * d],
            "back0": both[5:6, 2 * d : 3 * d],
            "back1": both[3:4, 0:d],
            "pool": both[1:2, 3 * d : 4 * d],
        }
        for name, (row, lane, size) in small_layout(m, kw, d, ff).items():
            for b in range(m):
                if name == "slopes":
                    table[b * SMALL + row : b * SMALL + row + 1, 0:heads] = slope_row[:, 0:heads]
                    table[b * SMALL + row : b * SMALL + row + 1, heads : 2 * heads] = both[3:4, d : d + heads]
                    continue
                for at in range(0, size, kw):
                    span = min(kw, size - at)
                    spot = b * SMALL + row + at // kw
                    first = b * size + at
                    table[spot : spot + 1, lane : lane + span] = vectors[name][:, first : first + span]
        pooled_ref = pooled_ref.get()
        for i in range(3):
            early, _ = pool_unit(3 * s + i, n, d)
            pool[i * d : (i + 1) * d, :] = flip(tn(groups[i], pooled_ref[early.astype(jnp.int32)]).astype(BF))
        for k in range(n):
            shares[k][0 : 3 * dh, :] = owners[s ^ k]
            shares[k][3 * dh :, :] = table[...].astype(BF)

    outs = [((3 * dh + m * SMALL, kw), BF)] * n + [((3 * rows, dh), BF)] * n + [((3 * d, kw), BF)]
    scratch = (
        attend_scratch(length, width, head_count)
        + [
            pltpu.VMEM((length, width), BF),
            pltpu.VMEM((3 * width, length), BF),
            pltpu.VMEM((n, 3 * dh, kw), BF),
            pltpu.VMEM((m * SMALL, kw), F32),
            pltpu.VMEM((3, n * third, kw), BF),
        ]
        + back_scratch(length, width, head_count)
    )
    result = call(
        body,
        "first_attention_back",
        [idx, slopes, qkv, attn, mixt, lse, *grads, wq, lnp, small_short, small_ffn, pooled_grad],
        [smem(), smem()] + [held(n)] * 4 + [NEAR] * n + [ALL, NEAR, held(n), held(n), held(n)],
        outs,
        scratch,
        after=after,
    )
    return result[:n], result[n : 2 * n], result[2 * n]


def input_gradient(idx, pieces, w_qkv, hid, middle_grad, lnp, after):
    n = len(pieces)
    dh = pieces[0].shape[1]
    rows, d = hid.shape

    def body(*refs):
        idx_ref = refs[0]
        piece_refs = refs[1 : 1 + n]
        w_ref, hid_ref, mid_ref, ln_ref, out, owners, whole, back = refs[1 + n :]
        s = idx_ref[0]
        for k in range(n):
            owners[s ^ k] = piece_refs[k][0 : 3 * rows, :]
        for j in range(n):
            for g in range(3):
                whole[:, g * d + j * dh : g * d + (j + 1) * dh] = owners[j, g * rows : (g + 1) * rows, :]
        back[...] = nt(whole[...], w_ref.get()[...])
        hid_ref, mid_ref = hid_ref.get(), mid_ref.get()

        def put(tile, value):
            out.ref[tile, :] = mid_ref[tile, :] + value

        norm_back(
            lambda tile: hid_ref[tile, :].astype(F32), ln_ref[0:1, :], lambda tile: back[tile, :], put, rows
        )

    scratch = [pltpu.VMEM((n, 3 * rows, dh), BF), pltpu.VMEM((rows, 3 * d), BF), pltpu.VMEM((rows, d), F32)]
    return call(
        body,
        "input_gradient",
        [idx, *pieces, w_qkv, hid, middle_grad, lnp],
        [smem()] + [NEAR] * n + [0, ALL, held(n), NEAR],
        [((rows, d), F32, FAR)],
        scratch,
        after=after,
        weight=0,
    )[0]


def order_shares(idx, pieces, pool, m, d, after):
    n = len(pieces)
    kw = pieces[0].shape[1]
    per, block, blocks = last_layout(n, m, d)
    every = per + block * blocks + SMALL
    dh = kw

    def body(*refs):
        idx_ref = refs[0]
        piece_refs = refs[1 : 1 + n]
        pool_ref, keep, give_near, give_far, natural, table = refs[1 + n :]
        s, mine = idx_ref[0], idx_ref[1]
        total = jnp.zeros((m * SMALL, kw), F32)
        for k in range(n):
            for g in range(3):
                at = g * dh
                natural[rows_at(g * d + (s ^ k) * dh, dh), :] = piece_refs[k][at : at + dh, :]
            total = total + piece_refs[k][3 * dh :, :].astype(F32)
        table[...] = total.astype(BF)
        for rel in range(m):
            target = (give_far if rel >= m // 2 else give_near) if rel & 1 else keep
            at = ((rel >> 1) % (m // 4) if rel & 1 else rel >> 1) * every
            b = mine ^ rel
            target[at : at + per, :] = natural[rows_at(b * per, per), :]
            for i in range(blocks):
                here = slice(at + per + i * block, at + per + (i + 1) * block)
                target[here, :] = pool_ref[rows_at(i * d + b * block, block), :]
            target[at + every - SMALL : at + every, :] = table[rows_at(b * SMALL, SMALL), :]

    return call(
        body,
        "order_shares",
        [idx, *pieces, pool],
        [smem()] + [NEAR] * (n + 1),
        [((m // 2 * every, kw), BF)] + [((m // 4 * every, kw), BF)] * 2,
        [pltpu.VMEM((3 * d, kw), BF), pltpu.VMEM((m * SMALL, kw), BF)],
        after=after,
    )


def unpack(held, spans, which, kw, n, qkv, out, inner, back):
    for j in range(n):
        lanes = slice(j * kw, (j + 1) * kw)
        for name, target in (("qkv", qkv), ("out", out)):
            at, count, _ = spans[name]
            target[:, lanes] = held[j, at : at + count, :].astype(F32)
        at, count, blocks = spans["in"]
        for i in range(blocks):
            inner[lanes, i * kw : (i + 1) * kw] = held[j, at + i * count : at + (i + 1) * count, :].astype(F32)
        at, count, blocks = spans["back"]
        for i in range(blocks):
            first = (j * blocks + i) * kw
            back[:, first : first + kw] = held[j, at + i * count : at + (i + 1) * count, :].astype(F32)


def both_layers(n, m, d, ff, which):
    shapes = ((2, 3 * d // m, d), (2, d // m, d), (2, d, ff // m), (2, d // m, ff))
    return [(shape, F32, PART, which) for shape in shapes]


def finish_short(idx, parts, skip, small, n, m, d, ff, heads, after):
    kw = d // n
    spans, _ = short_layout(n, m, d, ff)

    def body(*refs):
        idx_ref, part_refs, small = refs[0], refs[1 : 1 + n], refs[1 + n]
        qkv, out, inner, back, up = refs[2 + n : 7 + n]
        gains, biases, slopes, in_bias, back_bias, pool_bias, up_bias, held = refs[7 + n :]
        s = idx_ref[0]
        for k in range(n):
            held[s ^ k] = part_refs[k][skip if k else 0 :, :]
        unpack(held, spans, 1, kw, n, qkv.ref, out.ref, inner.ref, back.ref)
        for target in (qkv, out, inner, back):
            target.send()
        for j in range(n):
            at, count, _ = spans["up"]
            up.ref[:, j * kw : (j + 1) * kw] = held[j, at : at + count, :].astype(F32)
        up.send()
        places = small_layout(m, kw, d, ff)

        def pick(name, count):
            row, lane, _ = places[name]
            return small[row : row + 1, lane : lane + count]

        for which in range(2):
            for norm_at in range(2):
                name = str(which) + str(norm_at)
                gains[which, norm_at : norm_at + 1, :] = pick("gain" + name, d // m)
                biases[which, norm_at : norm_at + 1, :] = pick("bias" + name, d // m)
            back_bias[which : which + 1, :] = pick("back" + str(which), d // m)
            row = places["slopes"][0]
            slopes[which : which + 1, :] = small[row : row + 1, which * heads : (which + 1) * heads]
        pool_bias[...] = pick("pool", d // m)
        for at in range(0, ff // m, kw):
            for which in range(2):
                row = places["in" + str(which)][0] + at // kw
                in_bias[which : which + 1, at : at + kw] = small[row : row + 1, :]
        for at in range(0, 3 * d // m, kw):
            span = min(kw, 3 * d // m - at)
            row = places["up"][0] + at // kw
            up_bias[:, at : at + span] = small[row : row + 1, 0:span]

    outs = both_layers(n, m, d, ff, 1) + [
        ((3 * d // m, d), F32, FAR),
        ((2, 2, d // m), F32),
        ((2, 2, d // m), F32),
        ((2, heads), F32),
        ((2, ff // m), F32),
        ((2, d // m), F32),
        ((1, d // m), F32),
        ((1, 3 * d // m), F32),
    ]
    return call(
        body,
        "finish_short",
        [idx, *parts, small],
        [smem()] + [NEAR] * (n + 1),
        outs,
        [pltpu.VMEM((n,) + parts[0].shape, BF)],
        after=after,
        weight=0,
    )


def finish_first(idx, parts, begun, n, m, d, ff):
    kw = d // n
    spans, rows = ffn_layout(n, m, d, ff)
    per, block, blocks = last_layout(n, m, d)
    spans = dict(spans, qkv=(rows, per, 1), pool=(rows + per, block, blocks))

    def body(*refs):
        idx_ref, part_refs = refs[0], refs[1 : 1 + n]
        qkv, out, inner, back, pool, held = refs[5 + n :]
        s = idx_ref[0]
        for k in range(n):
            held[s ^ k] = part_refs[k][...]
        unpack(held, spans, 0, kw, n, qkv.ref, out.ref, inner.ref, back.ref)
        for target in (qkv, out, inner, back):
            target.send()
        for j in range(n):
            at, count, blocks = spans["pool"]
            for i in range(blocks):
                first = (j * blocks + i) * kw
                pool.ref[:, first : first + kw] = held[j, at + i * count : at + (i + 1) * count, :].astype(F32)
        pool.send()

    outs = both_layers(n, m, d, ff, 0) + [((d // m, 3 * d), F32, FAR)]
    return call(
        body,
        "finish_first",
        [idx, *parts, *begun],
        [smem()] + [NEAR] * n + [RAW] * 4,
        outs,
        [pltpu.VMEM((n,) + parts[0].shape, BF)],
        aliases={n + 1 + i: i for i in range(4)},
    )


def swap(array, axis, by):
    count = lax.axis_size(axis)
    return lax.ppermute(array, axis, [(i, i ^ by) for i in range(count)])


def gather(array, axis):
    return [array] + [swap(array, axis, k) for k in range(1, lax.axis_size(axis))]


def exchange(arrays, axis):
    return [arrays[0]] + [swap(arrays[k], axis, k) for k in range(1, len(arrays))]


def local(
    hidden_in, out_grad, start_flags, ln_gain, ln_bias, w_qkv, w_out, slopes, w_in, b_in, w_back, b_back,
    w_pool, b_pool, w_up, b_up,
):
    n, m = lax.axis_size("seq"), lax.axis_size("batch")
    s, mine = lax.axis_index("seq"), lax.axis_index("batch")
    idx = jnp.stack([s, mine]).astype(jnp.int32)
    hid = hidden_in[0]
    rows, d = hid.shape
    ff = w_in.shape[2]
    heads = slopes.shape[1]
    head_count = heads // n
    dh = head_count * HEAD
    width = max(dh, 128)
    far = m // 2
    row = lambda v: v.astype(F32).reshape(1, -1)

    hidden_parts = gather(hid, "seq")
    lnp = jnp.concatenate([ln_gain.reshape(4, d), ln_bias.reshape(4, d)], axis=0).astype(F32)
    columns = [lax.dynamic_slice(w_qkv, (0, 0, g * d + s * dh), (1, d, dh))[0] for g in range(3)]
    wq = jnp.concatenate([jnp.pad(c, ((0, 0), (0, width - dh))) for c in columns], axis=1)
    early = first_rows([hid, hidden_parts[n - 1]], wq, lnp)
    given = mask_rows(out_grad[0], start_flags[0][:, None], [*hidden_parts[1:], early[1]])
    given_parts = [swap(given, "seq", k) for k in range(1, n - 1)]

    loaded = [(w_out, 0), (w_in, 0), (w_back, 0), (w_up, None), (w_back, 1)] if keeps(n) else []
    sends, (attn, qkv, mixt, lse), loaded = first_attention(
        idx, slopes, [None, *hidden_parts[1 : n - 1], None], early, wq, lnp, loaded, head_count, dh, [given]
    )
    fetched = loaded[3:]
    loaded = loaded[:3] or [w_out, w_in, w_back]
    mixes = exchange(sends, "seq")
    given = pass_on(given, [*mixes[1:], *given_parts])
    last_given = swap(given, "seq", n - 1)
    full_g, pooled, mid, forward, rate = first_ffn(
        idx, hid, mixes, lnp, loaded[0], loaded[1], row(b_in[0]), loaded[2], row(b_back[0]), w_pool, row(b_pool),
        [given],
    )
    pooled_parts = gather(pooled, "seq")
    forward_other = swap(forward, "batch", 1)
    given_parts = [given] + given_parts + [last_given]
    begun, up_held, back_held, short_weights = [], w_up, w_back, [w_qkv, w_out, w_in, w_pool]
    if keeps(n):
        up_held, back_held = fetched
        result = short_start(idx, given_parts, up_held, back_held, short_weights[:3], w_pool, [mid])
        begun, short_weights = result[:4], result[4:]
    block_out, full_grad, pair, keep, give, small_short = short_layer(
        idx, slopes, pooled_parts, given_parts, begun, full_g, lnp, *short_weights[:3], row(b_in[1]), back_held,
        row(b_back[1]), short_weights[3], up_held, row(b_up), m, [],
    )

    short_rows = keep.shape[1]
    keep, give = keep.reshape(-1, keep.shape[2]), give.reshape(-1, keep.shape[2])
    other = swap(give, "batch", 1)
    sends, (middle_grad, back, give, small_ffn, *fetched) = first_ffn_back(
        idx, full_grad, mid, rate, forward, lnp, *loaded, [forward_other] if keeps(n) else [], n, m
    )
    forward_other = fetched[0] if fetched else forward_other
    back_other = swap(give, "batch", 1)
    grads = exchange(sends, "seq")

    def split(parts, count, size, places):
        return [
            (BF, [[(part, i * size, size) for part in parts] for i in range(count) if places(i)]),
            (BF, [[(part, i * size, size) for part in parts] for i in range(count) if not places(i)]),
        ]

    even = lambda i: i % 2 == 0
    packs = first_ffn_weights(idx, forward, forward_other, back, back_other, n, m, d, ff, [])
    short_keep, short_give = fold("short_chip", split([keep, other], far, short_rows, even), [packs[0]])
    short_other = swap(short_give, "batch", 2)
    plan = halves(n, far)
    others = [swap(packs[2 * half + 1], "seq", bits[0]) for half, (bits, _) in enumerate(plan)]
    packs = [packs[0], packs[2]]
    shares, sends, pool = first_attention_back(
        idx, slopes, qkv, attn, mixt, lse, grads, wq, lnp, small_short, small_ffn, pair, head_count, dh, m, [short_keep]
    )
    shares = exchange(shares, "seq")

    size = ffn_layout(n, m, d, ff)[1]
    steps = n.bit_length() - 1
    short_count, after = far // 2, [shares[0]]
    for step in range(1, steps):
        targets, rest = [], []
        for (bits, places), pack, other in zip(plan, packs, others):
            orders = kept_orders(n, bits)[step]
            per = len(places) * size
            keeping = [i for i, r in enumerate(orders) if not r & bits[step]]
            targets += split([pack, other], len(orders), per, lambda i: i in keeping)
        if short_count > 1:
            targets += split([short_keep, short_other], short_count, short_rows, even)
        result = fold("first_plane", targets, after)
        packs, others = [result[0], result[2]], [result[1], result[3]]
        others = [swap(other, "seq", bits[step]) for (bits, _), other in zip(plan, others)]
        if short_count > 1:
            short_keep, short_other = result[4], swap(result[5], "batch", 2 * far // short_count)
            short_count //= 2
        after = [result[0]]
    while short_count > 1:
        short_keep, short_give = fold("short_plane", split([short_keep, short_other], short_count, short_rows, even))
        short_other = swap(short_give, "batch", 2 * far // short_count)
        short_count //= 2

    keep, *gives = order_shares(idx, shares, pool, m, d, after)
    last_rows = keep.shape[0] // far
    last_other = [swap(give, "batch", 1) for give in gives]
    short_sum = [(short_keep, 0, short_rows), (short_other, 0, short_rows)]

    def plane(z):
        half = z // (far // 2)
        at = (z - half * (far // 2)) * size
        return [(packs[half], at, size), (others[half], at, size)]

    def pieces(z):
        return [plane(z), [(keep, z * last_rows, last_rows), (last_other[2 * z // far], z % (far // 2) * last_rows, last_rows)]]

    short_total, result_keep, result_give, *messages = fold(
        "short_total",
        [(BF, [short_sum])]
        + [(BF, [block for z in range(far) if z % 2 == odd for block in pieces(z)]) for odd in range(2)]
        + [(BF, [[(sends[k], 0, sends[k].shape[0])], short_sum]) for k in range(1, n)],
        [keep],
    )
    both, count = size + last_rows, far // 2
    other = swap(result_give, "batch", 2)
    messages = [swap(message, "seq", k + 1) for k, message in enumerate(messages)]
    while count > 1:
        blocks = [[(part, i * both, both) for part in (result_keep, other)] for i in range(count)]
        result_keep, result_give = fold(
            "last_plane",
            [(BF, [blocks[i] for i in range(count) if i % 2 == odd]) for odd in range(2)],
            weight=0,
        )
        other = swap(result_give, "batch", 2 * far // count)
        count //= 2
    count = both - SMALL
    parts = [result_keep, other]
    first_total, smalls = fold(
        "first_total",
        [(BF, [[(part, 0, count) for part in parts]]), (F32, [[(part, count, SMALL) for part in parts]])],
        weight=0,
    )
    first_parts = gather(first_total, "seq")
    hidden_grad = input_gradient(idx, [sends[0], *messages], w_qkv, hid, middle_grad, lnp, [first_total])
    short_parts = [short_total, *messages]
    *begun, g_up, gains, biases, slope_grad, in_bias, back_bias, pool_bias, up_bias = finish_short(
        idx, short_parts, sends[0].shape[0], smalls, n, m, d, ff, heads, [in_hbm(hidden_grad)]
    )
    g_qkv, g_out, g_in, g_back, g_pool = finish_first(idx, first_parts, begun, n, m, d, ff)
    turn = lambda a: jnp.swapaxes(a, -1, -2)
    return (
        block_out[None],
        hidden_grad[None],
        gains,
        biases,
        turn(g_qkv),
        turn(g_out),
        slope_grad,
        g_in,
        in_bias,
        turn(g_back),
        back_bias,
        turn(g_pool),
        pool_bias[0],
        turn(g_up),
        up_bias[0],
    )


def solution(mesh):
    rows = P("batch", "seq", None)
    last = P(None, None, "batch")
    in_specs = (rows, rows, P("batch", "seq")) + (P(),) * 13
    out_specs = (
        rows,
        rows,
        last,
        last,
        last,
        last,
        P(),
        last,
        P(None, "batch"),
        last,
        P(None, "batch"),
        P(None, "batch"),
        P("batch"),
        P(None, "batch"),
        P("batch"),
    )
    return jax.shard_map(local, mesh=mesh, in_specs=in_specs, out_specs=out_specs, check_vma=False)
```

time: 912 us -> 189 us (0.21)
  waiting for transfers between devices: 563 us -> 39.8 us
  local copies, waits for them, and re-layouts: 101 us -> 4.29 us
  Pallas kernels: 0 us -> 91.9 us
  matrix products: 80.5 us -> 0 us
  blocking collectives: 62.4 us -> 0 us
  other arithmetic: 58.2 us -> 1.68 us
  starting transfers between devices: 17.3 us -> 46.3 us
  between operations: 17.2 us -> 1.17 us
    unnamed x20 -> x0, waiting for transfers between devices: 299 us -> none
    reduce_scatter x3 -> x0, waiting for transfers between devices: 116 us -> none  [the longest x1 50.9 us: local(): lax.psum_scatter(stacked[4].astype(jnp.bfloat16), 'batch', scatter_dimens...]
    pallas_call x0 -> x19, Pallas kernels: none -> 91.9 us  [call(): pl.pallas_call(kernel, out_shape=[shape_of[kind](out[0], out[1]) for out,...]
    all_gather x2 -> x0, waiting for transfers between devices: 86 us -> none  [the longest x1 44 us: fetch_full(): return lax.all_gather(key_rows, 'seq', axis=0, tiled=True)]
    dot_general x44 -> x0, matrix products: 80.5 us -> none  [the longest x2 7.73 us: layer_backward(): jnp.einsum('rd,fd->rf', branch_grad, w_back, preferred_element_type=jnp.f...]
    psum x1 -> x0, waiting for transfers between devices: 57.2 us -> none  [local(): lax.psum(for_sending(shards), 'seq')]
    psum x2 -> x0, blocking collectives: 48.3 us -> none  [the longest x1 38.2 us: local(): lax.psum(jnp.stack([full_grads[4], short_grads[4]]), ('seq', 'batch'))]
    unnamed x247 -> x12, local copies, waits for them, and re-layouts: 36.9 us -> 1.01 us
  transfers between devices with their start and end apart: 15 -> 37, of which waited for: 13 -> 15; matrix products, arithmetic and copies ran while one was open for 11% -> 3% of each run, Pallas kernels for 0% -> 46%
where the time goes in v1:
time: 189 us; the launch traced here: 185 us
  Pallas kernels  91.9 us (49%)
  starting transfers between devices  46.3 us (24%)
  waiting for transfers between devices  39.8 us (21%)
  local copies, waits for them, and re-layouts  4.29 us (2%)
    pallas_call x19, Pallas kernels, call(): pl.pallas_call(kernel, out_shape=[shape_of[kind](out[0], out[1]) for out,...  91.9 us
    ppermute x37, starting transfers between devices, swap(): return lax.ppermute(array, axis, [(i, i ^ by) for i in range(count)])  46.3 us
    ppermute x37, waiting for transfers between devices, swap(): return lax.ppermute(array, axis, [(i, i ^ by) for i in range(count)])  39.8 us
  transfers between devices with their start and end apart: 37, of which 15 were waited for; matrix products, arithmetic and copies ran while one was open for 3% of the time, Pallas kernels for 46%

profile of v1, /device:TPU:0, one launch (start us, length us, event | category | flops | bytes accessed | tf_op | source)
XLA Modules:
  0.0 185.1 jit_solution(16482901774591418582)
XLA Ops:
  0.6 4.0 %collective-permute-start.2 = (bf16[384,512]{1,0:T(8,128)(2,1)}, bf16[384,512]{1,0:T(8,128)(2,1)S(1)}, u32[]{:S(2)}, u32[]{:S(2)}) collective-permute-start(bf16[384,512]{1,0:T(8,128)(2,1)} %bitcast.23), channel_id=1, source_target_pairs={{0,24},{8,16},{16,8},{24,0},{1,25},{9,17},{17,9},{25,1},{2,26},{10... | collective-permute-start | bytes 1179656 | tf_op jit(solution)/shard_map/ppermute | solution.py:1546
  10.2 4.6 %collective-permute-done.2.refs_1_.refs_4_ = bf16[384,512]{1,0:T(8,128)(2,1)S(1)} collective-permute-done((bf16[384,512]{1,0:T(8,128)(2,1)}, bf16[384,512]{1,0:T(8,128)(2,1)S(1)}, u32[]{:S(2)}, u32[]{:S(2)}) %collective-permute-start.2) | collective-permute-done | bytes 393248 | tf_op jit(solution)/shard_map/ppermute | solution.py:1546
  15.8 1.7 first_rows.1
  17.5 5.1 %collective-permute-done.refs_2_ = bf16[384,512]{1,0:T(8,128)(2,1)S(1)} collective-permute-done((bf16[384,512]{1,0:T(8,128)(2,1)}, bf16[384,512]{1,0:T(8,128)(2,1)S(1)}, u32[]{:S(2)}, u32[]{:S(2)}) %collective-permute-start) | collective-permute-done | bytes 393248 | tf_op jit(solution)/shard_map/ppermute | solution.py:1546
  22.9 1.6 collective-permute-start.6
  25.8 11.2 %first_attention.1 = (bf16[384,128]{1,0:T(8,128)(2,1)S(1)}, bf16[384,128]{1,0:T(8,128)(2,1)S(1)}, bf16[384,128]{1,0:T(8,128)(2,1)S(1)}, bf16[384,128]{1,0:T(8,12...) custom-call(s32[2]{0:T(128)S(1)} %pad_add_fusion.refs_0_, ...), custom_call_target="tpu_custom_call" | custom-call | flops 10000000000 | tf_op jit(solution)/shard_map/first_attention/pallas_call | solution.py:432
  38.3 2.3 %collective-permute-start.5 = (bf16[384,128]{1,0:T(8,128)(2,1)S(1)}, bf16[384,128]{1,0:T(8,128)(2,1)S(1)}, u32[]{:S(2)}, u32[]{:S(2)}) collective-permute-start(bf16[384,128]{1,0:T(8,128)(2,1)S(1)} %get-tuple-element.114), channel_id=1, source_target_pairs={{0,24},{8,16},{16,8},{24,0},{1,25},{9,17},{17,9},{25,1},{2,26},{10... | collective-permute-start | bytes 294920 | tf_op jit(solution)/shard_map/ppermute | solution.py:1546
  40.7 2.0 %collective-permute-done.3.refs_1_.refs_3_ = bf16[384,128]{1,0:T(8,128)(2,1)S(1)} collective-permute-done((bf16[384,128]{1,0:T(8,128)(2,1)S(1)}, bf16[384,128]{1,0:T(8,128)(2,1)S(1)}, u32[]{:S(2)}, u32[]{:S(2)}) %collective-permute-start.3) | collective-permute-done | bytes 98336 | tf_op jit(solution)/shard_map/ppermute | solution.py:1546
  43.9 2.3 %collective-permute-start.11 = (bf16[128,1536]{1,0:T(8,128)(2,1)S(1)}, bf16[128,1536]{1,0:T(8,128)(2,1)S(1)}, u32[]{:S(2)}, u32[]{:S(2)}) collective-permute-start(bf16[128,1536]{1,0:T(8,128)(2,1)S(1)} %pass_on.1.refs_14_.refs_1_), channel_id=1, source_target_pairs={{0,24},{8,16},{16,8},{24,0},{1,25},{9,17},{17,9},{25,1},{2,26},{10... | collective-permute-start | bytes 1179656 | tf_op jit(solution)/shard_map/ppermute | solution.py:1546
  46.2 6.1 %first_ffn.1 = (f32[128,1536]{1,0:T(8,128)S(1)}, bf16[144,512]{1,0:T(8,128)(2,1)S(1)}, f32[384,512]{1,0:T(8,128)S(1)}, bf16[512,3072]{1,0:T(8,128)(2,1)S(1)}, bf16[384,2048]{1,0:T(8,128)(2,1)S(1)}) custom-call(s32[2]{0:T(128)S(1)} %pad_add_fusion.refs_0_, bf16[384,512]{1,0:T(8,128)(2,1)} %bitcast.26, bf16[384,128]{1,0:T(8,128)(2,1)S(1)} %get-tuple-element.111.refs_2_, ...), custom_call_target="tpu_custom_call" | custom-call | flops 10000000000 | tf_op jit(solution)/shard_map/first_ffn/pallas_call | solution.py:432
  53.1 1.6 collective-permute-start.8
  55.9 4.1 %short_start.1 = (bf16[512,1536]{1,0:T(8,128)(2,1)S(1)}, f32[512,512]{1,0:T(8,128)S(1)}, bf16[512,512]{1,0:T(8,128)(2,1)S(1)}, bf16[512,2048]{1,0:T(8,128)(2,1)S...) custom-call(s32[2]{0:T(128)S(1)} %pad_add_fusion.refs_0_, ...), custom_call_target="tpu_custom_call" | custom-call | flops 99999997952 | tf_op jit(solution)/shard_map/short_start/pallas_call | solution.py:432
  60.8 37.9 %short_layer.1 = (bf16[384,512]{1,0:T(8,128)(2,1)}, f32[384,512]{1,0:T(8,128)S(1)}, bf16[2,512,512]{2,1,0:T(8,128)(2,1)S(1)}, bf16[4,960,128]{2,1,0:T(8,128)(2,1...) custom-call(s32[2]{0:T(128)S(1)} %pad_add_fusion.refs_0_, f32[2,8]{1,0:T(2,128)S(1)} %copy-done.2, ...), custom_call_target="tpu_custom_call" | custom-call | flops 10000000000 | tf_op jit(solution)/shard_map/short_layer/pallas_call | solution.py:432
  98.8 4.5 %first_ffn_back.1 = (bf16[768,128]{1,0:T(8,128)(2,1)S(1)}, bf16[768,128]{1,0:T(8,128)(2,1)S(1)}, bf16[768,128]{1,0:T(8,128)(2,1)S(1)}, bf16[768,128]{1,0:T(8,128...) custom-call(s32[2]{0:T(128)S(1)} %pad_add_fusion.refs_0_, ...), custom_call_target="tpu_custom_call" | custom-call | flops 10000000000 | tf_op jit(solution)/shard_map/first_ffn_back/pallas_call | solution.py:432
  104.6 1.4 collective-permute-start.14
  107.3 3.7 %first_ffn_weights.1 = (bf16[2304,128]{1,0:T(8,128)(2,1)S(1)}, bf16[2304,128]{1,0:T(8,128)(2,1)S(1)}, bf16[2304,128]{1,0:T(8,128)(2,1)S(1)}, bf16[2304,128]{1,0:T(8,128)(2,1)S(1)}) custom-call(s32[2]{0:T(128)S(1)} %pad_add_fusion.refs_0_, bf16[512,3072]{1,0:T(8,128)(2,1)S(1)} %get-tuple-element.138.refs_4_.refs_1_, ...), custom_call_target="tpu_custom_call" | custom-call | flops 10000000000 | tf_op jit(solution)/shard_map/first_ffn_weights/pallas_call | solution.py:432
  111.3 1.6 collective-permute-start.20
  116.1 10.8 %first_attention_back.1 = (bf16[512,128]{1,0:T(8,128)(2,1)S(1)}, bf16[512,128]{1,0:T(8,128)(2,1)S(1)}, bf16[512,128]{1,0:T(8,128)(2,1)S(1)}, bf16[512,128]{1,0:T...) custom-call(s32[2]{0:T(128)S(1)} %pad_add_fusion.refs_0_, ...), custom_call_target="tpu_custom_call" | custom-call | flops 10000000000 | tf_op jit(solution)/shard_map/first_attention_back/pallas_call | solution.py:432
  127.9 1.4 collective-permute-start.24
  131.8 1.5 collective-permute-start.27
  133.3 2.6 %collective-permute-start.21 = (bf16[960,128]{1,0:T(8,128)(2,1)S(1)}, bf16[960,128]{1,0:T(8,128)(2,1)S(1)}, u32[]{:S(2)}, u32[]{:S(2)}) collective-permute-start(bf16[960,128]{1,0:T(8,128)(2,1)S(1)} %get-tuple-element.160), channel_id=1, source_target_pairs={{0,4},{1,5},{2,6},{3,7},{4,0},{5,1},{6,2},{7,3},{8,12},{9,13},{10,... | collective-permute-start | bytes 737288 | tf_op jit(solution)/shard_map/ppermute | solution.py:1546
  139.1 4.9 %collective-permute-done.21.refs_1_ = bf16[960,128]{1,0:T(8,128)(2,1)S(1)} collective-permute-done((bf16[960,128]{1,0:T(8,128)(2,1)S(1)}, bf16[960,128]{1,0:T(8,128)(2,1)S(1)}, u32[]{:S(2)}, u32[]{:S(2)}) %collective-permute-start.21) | collective-permute-done | bytes 245792 | tf_op jit(solution)/shard_map/ppermute | solution.py:1546
  148.7 6.3 %collective-permute-done.32.refs_1_ = bf16[1952,128]{1,0:T(8,128)(2,1)S(1)} collective-permute-done((bf16[1952,128]{1,0:T(8,128)(2,1)S(1)}, bf16[1952,128]{1,0:T(8,128)(2,1)S(1)}, u32[]{:S(2)}, u32[]{:S(2)}) %collective-permute-start.32) | collective-permute-done | bytes 499744 | tf_op jit(solution)/shard_map/ppermute | solution.py:1546
  155.1 3.4 %collective-permute-start.33 = (bf16[976,128]{1,0:T(8,128)(2,1)S(1)}, bf16[976,128]{1,0:T(8,128)(2,1)S(1)}, u32[]{:S(2)}, u32[]{:S(2)}) collective-permute-start(bf16[976,128]{1,0:T(8,128)(2,1)S(1)} %get-tuple-element.182), channel_id=1, source_target_pairs={{0,4},{1,5},{2,6},{3,7},{4,0},{5,1},{6,2},{7,3},{8,12},{9,13},{10,... | collective-permute-start | bytes 749576 | tf_op jit(solution)/shard_map/ppermute | solution.py:1546
  158.6 9.1 %collective-permute-done.33.refs_1_ = bf16[976,128]{1,0:T(8,128)(2,1)S(1)} collective-permute-done((bf16[976,128]{1,0:T(8,128)(2,1)S(1)}, bf16[976,128]{1,0:T(8,128)(2,1)S(1)}, u32[]{:S(2)}, u32[]{:S(2)}) %collective-permute-start.33) | collective-permute-done | bytes 249888 | tf_op jit(solution)/shard_map/ppermute | solution.py:1546
  167.7 2.1 %collective-permute-start.34 = (bf16[960,128]{1,0:T(8,128)(2,1)S(1)}, bf16[960,128]{1,0:T(8,128)(2,1)S(1)}, u32[]{:S(2)}, u32[]{:S(2)}) collective-permute-start(bf16[960,128]{1,0:T(8,128)(2,1)S(1)} %get-tuple-element.183.refs_9_.refs_1_), channel_id=1, source_target_pairs={{0,8},{8,0},{16,24},{24,16},{1,9},{9,1},{17,25},{25,17},{2,10},{10... | collective-permute-start | bytes 737288 | tf_op jit(solution)/shard_map/ppermute | solution.py:1546
  169.9 1.5 collective-permute-start.35
  172.4 4.2 %input_gradient.1.refs_6_ = f32[384,512]{1,0:T(8,128)} custom-call(s32[2]{0:T(128)S(1)} %pad_add_fusion.refs_0_, bf16[1152,128]{1,0:T(8,128)(2,1)S(1)} %get-tuple-element.153.refs_1_, bf16[2112,128]{1,0:T(8,128)(2,1)S(1)} %collective-permute-done.29.refs_2_, bf16[2112,128]{1,0:T(8,128)(2,1)S(1)} %collective-permute-done.30.refs_3_, ...), custom_call_target="tpu_custom_call" | custom-call | tf_op jit(solution)/shard_map/input_gradient/pallas_call | solution.py:432
  176.6 3.0 %finish_short.1 = (f32[2,192,512]{2,1,0:T(8,128)}, f32[2,64,512]{2,1,0:T(8,128)}, f32[2,512,256]{2,1,0:T(8,128)}, f32[2,64,2048]{2,1,0:T(8,128)}, f32[192,512]{1...) custom-call(s32[2]{0:T(128)S(1)} %pad_add_fusion.refs_0_, ...), custom_call_target="tpu_custom_call" | custom-call | tf_op jit(solution)/shard_map/finish_short/pallas_call | solution.py:432
  179.6 1.4 collective-permute-done.35.refs_3_
  181.1 1.5 collective-permute-done.36.refs_4_
  182.5 2.3 %finish_first.1 = (f32[2,192,512]{2,1,0:T(8,128)}, f32[2,64,512]{2,1,0:T(8,128)}, f32[2,512,256]{2,1,0:T(8,128)}, f32[2,64,2048]{2,1,0:T(8,128)}, f32[64,1536]{1,0:T(8,128)}) custom-call(s32[2]{0:T(128)S(1)} %pad_add_fusion.refs_0_, ...), custom_call_target="tpu_custom_call", output_to_operand_aliasing={{0}: (5, {}), {1}: (6, {}), {2}: (7, {}), {3}: (8, {})} | custom-call | flops 10000000000 | tf_op jit(solution)/shard_map/finish_first/pallas_call | solution.py:432
  (84 shorter events, 31.9 us)
Async XLA Ops:
  0.6 14.2 %collective-permute-start.2 = (bf16[384,512]{1,0:T(8,128)(2,1)}, bf16[384,512]{1,0:T(8,128)(2,1)S(1)}, u32[]{:S(2)}, u32[]{:S(2)}) collective-permute-start(bf16[384,512]{1,0:T(8,128)(2,1)} %bitcast.23), channel_id=1, source_target_pairs={{0,24},{8,16},{16,8},{24,0},{1,25},{9,17},{17,9},{25,1},{2,26},{10... | collective-permute-start | bytes 1179656 | tf_op jit(solution)/shard_map/ppermute | solution.py:1546
  4.6 18.0 %collective-permute-start = (bf16[384,512]{1,0:T(8,128)(2,1)}, bf16[384,512]{1,0:T(8,128)(2,1)S(1)}, u32[]{:S(2)}, u32[]{:S(2)}) collective-permute-start(bf16[384,512]{1,0:T(8,128)(2,1)} %bitcast.24), channel_id=1, source_target_pairs={{0,8},{8,0},{16,24},{24,16},{1,9},{9,1},{17,25},{25,17},{2,10},{10... | collective-permute-start | bytes 1179656 | tf_op jit(solution)/shard_map/ppermute | solution.py:1546
  5.1 17.5 %collective-permute-start.1 = (bf16[384,512]{1,0:T(8,128)(2,1)}, bf16[384,512]{1,0:T(8,128)(2,1)S(1)}, u32[]{:S(2)}, u32[]{:S(2)}) collective-permute-start(bf16[384,512]{1,0:T(8,128)(2,1)} %bitcast.25), channel_id=1, source_target_pairs={{0,16},{8,24},{16,0},{24,8},{1,17},{9,25},{17,1},{25,9},{2,18},{10... | collective-permute-start | bytes 1179656 | tf_op jit(solution)/shard_map/ppermute | solution.py:1546
  22.9 21.0 %collective-permute-start.6 = (bf16[128,1536]{1,0:T(8,128)(2,1)S(1)}, bf16[128,1536]{1,0:T(8,128)(2,1)S(1)}, u32[]{:S(2)}, u32[]{:S(2)}) collective-permute-start(bf16[128,1536]{1,0:T(8,128)(2,1)S(1)} %mask_rows.1.refs_13_.refs_0_), channel_id=1, source_target_pairs={{0,8},{8,0},{16,24},{24,16},{1,9},{9,1},{17,25},{25,17},{2,10},{10... | collective-permute-start | bytes 1179656 | tf_op jit(solution)/shard_map/ppermute | solution.py:1546
  24.4 19.4 %collective-permute-start.7 = (bf16[128,1536]{1,0:T(8,128)(2,1)S(1)}, bf16[128,1536]{1,0:T(8,128)(2,1)S(1)}, u32[]{:S(2)}, u32[]{:S(2)}) collective-permute-start(bf16[128,1536]{1,0:T(8,128)(2,1)S(1)} %mask_rows.1.refs_13_.refs_0_), channel_id=1, source_target_pairs={{0,16},{8,24},{16,0},{24,8},{1,17},{9,25},{17,1},{25,9},{2,18},{10... | collective-permute-start | bytes 1179656 | tf_op jit(solution)/shard_map/ppermute | solution.py:1546
  37.0 5.7 %collective-permute-start.3 = (bf16[384,128]{1,0:T(8,128)(2,1)S(1)}, bf16[384,128]{1,0:T(8,128)(2,1)S(1)}, u32[]{:S(2)}, u32[]{:S(2)}) collective-permute-start(bf16[384,128]{1,0:T(8,128)(2,1)S(1)} %get-tuple-element.112), channel_id=1, source_target_pairs={{0,8},{8,0},{16,24},{24,16},{1,9},{9,1},{17,25},{25,17},{2,10},{10... | collective-permute-start | bytes 294920 | tf_op jit(solution)/shard_map/ppermute | solution.py:1546
  43.9 12.0 %collective-permute-start.11 = (bf16[128,1536]{1,0:T(8,128)(2,1)S(1)}, bf16[128,1536]{1,0:T(8,128)(2,1)S(1)}, u32[]{:S(2)}, u32[]{:S(2)}) collective-permute-start(bf16[128,1536]{1,0:T(8,128)(2,1)S(1)} %pass_on.1.refs_14_.refs_1_), channel_id=1, source_target_pairs={{0,24},{8,16},{16,8},{24,0},{1,25},{9,17},{17,9},{25,1},{2,26},{10... | collective-permute-start | bytes 1179656 | tf_op jit(solution)/shard_map/ppermute | solution.py:1546
  52.4 7.7 %collective-permute-start.10 = (bf16[144,512]{1,0:T(8,128)(2,1)S(1)}, bf16[144,512]{1,0:T(8,128)(2,1)S(1)}, u32[]{:S(2)}, u32[]{:S(2)}) collective-permute-start(bf16[144,512]{1,0:T(8,128)(2,1)S(1)} %get-tuple-element.118.refs_2_), channel_id=1, source_target_pairs={{0,24},{8,16},{16,8},{24,0},{1,25},{9,17},{17,9},{25,1},{2,26},{10... | collective-permute-start | bytes 442376 | tf_op jit(solution)/shard_map/ppermute | solution.py:1546
  53.1 7.7 %collective-permute-start.8 = (bf16[144,512]{1,0:T(8,128)(2,1)S(1)}, bf16[144,512]{1,0:T(8,128)(2,1)S(1)}, u32[]{:S(2)}, u32[]{:S(2)}) collective-permute-start(bf16[144,512]{1,0:T(8,128)(2,1)S(1)} %get-tuple-element.118.refs_2_), channel_id=1, source_target_pairs={{0,8},{8,0},{16,24},{24,16},{1,9},{9,1},{17,25},{25,17},{2,10},{10... | collective-permute-start | bytes 442376 | tf_op jit(solution)/shard_map/ppermute | solution.py:1546
  54.7 6.1 %collective-permute-start.9 = (bf16[144,512]{1,0:T(8,128)(2,1)S(1)}, bf16[144,512]{1,0:T(8,128)(2,1)S(1)}, u32[]{:S(2)}, u32[]{:S(2)}) collective-permute-start(bf16[144,512]{1,0:T(8,128)(2,1)S(1)} %get-tuple-element.118.refs_2_), channel_id=1, source_target_pairs={{0,16},{8,24},{16,0},{24,8},{1,17},{9,25},{17,1},{25,9},{2,18},{10... | collective-permute-start | bytes 442376 | tf_op jit(solution)/shard_map/ppermute | solution.py:1546
  55.9 42.8 %collective-permute-start.12 = (bf16[512,3072]{1,0:T(8,128)(2,1)S(1)}, bf16[512,3072]{1,0:T(8,128)(2,1)S(1)}, u32[]{:S(2)}, u32[]{:S(2)}) collective-permute-start(bf16[512,3072]{1,0:T(8,128)(2,1)S(1)} %get-tuple-element.138.refs_4_.refs_1_), channel_id=1, source_target_pairs={{0,1},{1,0},{2,3},{3,2},{4,5},{5,4},{6,7},{7,6},{8,9},{9,8},{10,11... | collective-permute-start | bytes 9437192 | tf_op jit(solution)/shard_map/ppermute | solution.py:1546
  103.3 7.7 %collective-permute-start.16 = (bf16[3840,128]{1,0:T(8,128)(2,1)S(1)}, bf16[3840,128]{1,0:T(8,128)(2,1)S(1)}, u32[]{:S(2)}, u32[]{:S(2)}) collective-permute-start(bf16[3840,128]{1,0:T(8,128)(2,1)S(1)} %bitcast.30), channel_id=1, source_target_pairs={{0,1},{1,0},{2,3},{3,2},{4,5},{5,4},{6,7},{7,6},{8,9},{9,8},{10,11... | collective-permute-start | bytes 2949128 | tf_op jit(solution)/shard_map/ppermute | solution.py:1546
  103.8 9.9 %collective-permute-start.13 = (bf16[768,128]{1,0:T(8,128)(2,1)S(1)}, bf16[768,128]{1,0:T(8,128)(2,1)S(1)}, u32[]{:S(2)}, u32[]{:S(2)}) collective-permute-start(bf16[768,128]{1,0:T(8,128)(2,1)S(1)} %get-tuple-element.140), channel_id=1, source_target_pairs={{0,8},{8,0},{16,24},{24,16},{1,9},{9,1},{17,25},{25,17},{2,10},{10... | collective-permute-start | bytes 589832 | tf_op jit(solution)/shard_map/ppermute | solution.py:1546
  104.6 10.5 %collective-permute-start.14 = (bf16[768,128]{1,0:T(8,128)(2,1)S(1)}, bf16[768,128]{1,0:T(8,128)(2,1)S(1)}, u32[]{:S(2)}, u32[]{:S(2)}) collective-permute-start(bf16[768,128]{1,0:T(8,128)(2,1)S(1)} %get-tuple-element.141), channel_id=1, source_target_pairs={{0,16},{8,24},{16,0},{24,8},{1,17},{9,25},{17,1},{25,9},{2,18},{10... | collective-permute-start | bytes 589832 | tf_op jit(solution)/shard_map/ppermute | solution.py:1546
  106.0 10.1 %collective-permute-start.15 = (bf16[768,128]{1,0:T(8,128)(2,1)S(1)}, bf16[768,128]{1,0:T(8,128)(2,1)S(1)}, u32[]{:S(2)}, u32[]{:S(2)}) collective-permute-start(bf16[768,128]{1,0:T(8,128)(2,1)S(1)} %get-tuple-element.142), channel_id=1, source_target_pairs={{0,24},{8,16},{16,8},{24,0},{1,25},{9,17},{17,9},{25,1},{2,26},{10... | collective-permute-start | bytes 589832 | tf_op jit(solution)/shard_map/ppermute | solution.py:1546
  111.3 18.1 %collective-permute-start.20 = (bf16[1920,128]{1,0:T(8,128)(2,1)S(1)}, bf16[1920,128]{1,0:T(8,128)(2,1)S(1)}, u32[]{:S(2)}, u32[]{:S(2)}) collective-permute-start(bf16[1920,128]{1,0:T(8,128)(2,1)S(1)} %get-tuple-element.157), channel_id=1, source_target_pairs={{0,2},{1,3},{2,0},{3,1},{4,6},{5,7},{6,4},{7,5},{8,10},{9,11},{10,... | collective-permute-start | bytes 1474568 | tf_op jit(solution)/shard_map/ppermute | solution.py:1546
  112.9 17.6 %collective-permute-start.18 = (bf16[2304,128]{1,0:T(8,128)(2,1)S(1)}, bf16[2304,128]{1,0:T(8,128)(2,1)S(1)}, u32[]{:S(2)}, u32[]{:S(2)}) collective-permute-start(bf16[2304,128]{1,0:T(8,128)(2,1)S(1)} %get-tuple-element.154), channel_id=1, source_target_pairs={{0,8},{8,0},{16,24},{24,16},{1,9},{9,1},{17,25},{25,17},{2,10},{10... | collective-permute-start | bytes 1769480 | tf_op jit(solution)/shard_map/ppermute | solution.py:1546
  113.7 16.8 %collective-permute-start.19 = (bf16[2304,128]{1,0:T(8,128)(2,1)S(1)}, bf16[2304,128]{1,0:T(8,128)(2,1)S(1)}, u32[]{:S(2)}, u32[]{:S(2)}) collective-permute-start(bf16[2304,128]{1,0:T(8,128)(2,1)S(1)} %get-tuple-element.156), channel_id=1, source_target_pairs={{0,16},{8,24},{16,0},{24,8},{1,17},{9,25},{17,1},{25,9},{2,18},{10... | collective-permute-start | bytes 1769480 | tf_op jit(solution)/shard_map/ppermute | solution.py:1546
  127.0 6.3 %collective-permute-start.23 = (bf16[512,128]{1,0:T(8,128)(2,1)S(1)}, bf16[512,128]{1,0:T(8,128)(2,1)S(1)}, u32[]{:S(2)}, u32[]{:S(2)}) collective-permute-start(bf16[512,128]{1,0:T(8,128)(2,1)S(1)} %get-tuple-element.163), channel_id=1, source_target_pairs={{0,8},{8,0},{16,24},{24,16},{1,9},{9,1},{17,25},{25,17},{2,10},{10... | collective-permute-start | bytes 393224 | tf_op jit(solution)/shard_map/ppermute | solution.py:1546
  127.9 8.0 %collective-permute-start.24 = (bf16[512,128]{1,0:T(8,128)(2,1)S(1)}, bf16[512,128]{1,0:T(8,128)(2,1)S(1)}, u32[]{:S(2)}, u32[]{:S(2)}) collective-permute-start(bf16[512,128]{1,0:T(8,128)(2,1)S(1)} %get-tuple-element.164), channel_id=1, source_target_pairs={{0,16},{8,24},{16,0},{24,8},{1,17},{9,25},{17,1},{25,9},{2,18},{10... | collective-permute-start | bytes 393224 | tf_op jit(solution)/shard_map/ppermute | solution.py:1546
  129.4 7.3 %collective-permute-start.25 = (bf16[512,128]{1,0:T(8,128)(2,1)S(1)}, bf16[512,128]{1,0:T(8,128)(2,1)S(1)}, u32[]{:S(2)}, u32[]{:S(2)}) collective-permute-start(bf16[512,128]{1,0:T(8,128)(2,1)S(1)} %get-tuple-element.165), channel_id=1, source_target_pairs={{0,24},{8,16},{16,8},{24,0},{1,25},{9,17},{17,9},{25,1},{2,26},{10... | collective-permute-start | bytes 393224 | tf_op jit(solution)/shard_map/ppermute | solution.py:1546
  130.9 13.0 %collective-permute-start.22 = (bf16[1152,128]{1,0:T(8,128)(2,1)S(1)}, bf16[1152,128]{1,0:T(8,128)(2,1)S(1)}, u32[]{:S(2)}, u32[]{:S(2)}) collective-permute-start(bf16[1152,128]{1,0:T(8,128)(2,1)S(1)} %get-tuple-element.162), channel_id=1, source_target_pairs={{0,16},{8,24},{16,0},{24,8},{1,17},{9,25},{17,1},{25,9},{2,18},{10... | collective-permute-start | bytes 884744 | tf_op jit(solution)/shard_map/ppermute | solution.py:1546
  131.8 12.1 %collective-permute-start.27 = (bf16[1152,128]{1,0:T(8,128)(2,1)S(1)}, bf16[1152,128]{1,0:T(8,128)(2,1)S(1)}, u32[]{:S(2)}, u32[]{:S(2)}) collective-permute-start(bf16[1152,128]{1,0:T(8,128)(2,1)S(1)} %get-tuple-element.170), channel_id=1, source_target_pairs={{0,8},{8,0},{16,24},{24,16},{1,9},{9,1},{17,25},{25,17},{2,10},{10... | collective-permute-start | bytes 884744 | tf_op jit(solution)/shard_map/ppermute | solution.py:1546
  133.3 10.6 %collective-permute-start.21 = (bf16[960,128]{1,0:T(8,128)(2,1)S(1)}, bf16[960,128]{1,0:T(8,128)(2,1)S(1)}, u32[]{:S(2)}, u32[]{:S(2)}) collective-permute-start(bf16[960,128]{1,0:T(8,128)(2,1)S(1)} %get-tuple-element.160), channel_id=1, source_target_pairs={{0,4},{1,5},{2,6},{3,7},{4,0},{5,1},{6,2},{7,3},{8,12},{9,13},{10,... | collective-permute-start | bytes 737288 | tf_op jit(solution)/shard_map/ppermute | solution.py:1546
  144.5 10.5 %collective-permute-start.32 = (bf16[1952,128]{1,0:T(8,128)(2,1)S(1)}, bf16[1952,128]{1,0:T(8,128)(2,1)S(1)}, u32[]{:S(2)}, u32[]{:S(2)}) collective-permute-start(bf16[1952,128]{1,0:T(8,128)(2,1)S(1)} %get-tuple-element.180), channel_id=1, source_target_pairs={{0,2},{1,3},{2,0},{3,1},{4,6},{5,7},{6,4},{7,5},{8,10},{9,11},{10,... | collective-permute-start | bytes 1499144 | tf_op jit(solution)/shard_map/ppermute | solution.py:1546
  145.2 26.2 %collective-permute-start.29 = (bf16[2112,128]{1,0:T(8,128)(2,1)S(1)}, bf16[2112,128]{1,0:T(8,128)(2,1)S(1)}, u32[]{:S(2)}, u32[]{:S(2)}) collective-permute-start(bf16[2112,128]{1,0:T(8,128)(2,1)S(1)} %get-tuple-element.175), channel_id=1, source_target_pairs={{0,8},{8,0},{16,24},{24,16},{1,9},{9,1},{17,25},{25,17},{2,10},{10... | collective-permute-start | bytes 1622024 | tf_op jit(solution)/shard_map/ppermute | solution.py:1546
  146.5 25.9 %collective-permute-start.30 = (bf16[2112,128]{1,0:T(8,128)(2,1)S(1)}, bf16[2112,128]{1,0:T(8,128)(2,1)S(1)}, u32[]{:S(2)}, u32[]{:S(2)}) collective-permute-start(bf16[2112,128]{1,0:T(8,128)(2,1)S(1)} %get-tuple-element.176), channel_id=1, source_target_pairs={{0,16},{8,24},{16,0},{24,8},{1,17},{9,25},{17,1},{25,9},{2,18},{10... | collective-permute-start | bytes 1622024 | tf_op jit(solution)/shard_map/ppermute | solution.py:1546
  147.9 24.5 %collective-permute-start.31 = (bf16[2112,128]{1,0:T(8,128)(2,1)S(1)}, bf16[2112,128]{1,0:T(8,128)(2,1)S(1)}, u32[]{:S(2)}, u32[]{:S(2)}) collective-permute-start(bf16[2112,128]{1,0:T(8,128)(2,1)S(1)} %get-tuple-element.177), channel_id=1, source_target_pairs={{0,24},{8,16},{16,8},{24,0},{1,25},{9,17},{17,9},{25,1},{2,26},{10... | collective-permute-start | bytes 1622024 | tf_op jit(solution)/shard_map/ppermute | solution.py:1546
  155.1 12.6 %collective-permute-start.33 = (bf16[976,128]{1,0:T(8,128)(2,1)S(1)}, bf16[976,128]{1,0:T(8,128)(2,1)S(1)}, u32[]{:S(2)}, u32[]{:S(2)}) collective-permute-start(bf16[976,128]{1,0:T(8,128)(2,1)S(1)} %get-tuple-element.182), channel_id=1, source_target_pairs={{0,4},{1,5},{2,6},{3,7},{4,0},{5,1},{6,2},{7,3},{8,12},{9,13},{10,... | collective-permute-start | bytes 749576 | tf_op jit(solution)/shard_map/ppermute | solution.py:1546
  167.7 11.9 %collective-permute-start.34 = (bf16[960,128]{1,0:T(8,128)(2,1)S(1)}, bf16[960,128]{1,0:T(8,128)(2,1)S(1)}, u32[]{:S(2)}, u32[]{:S(2)}) collective-permute-start(bf16[960,128]{1,0:T(8,128)(2,1)S(1)} %get-tuple-element.183.refs_9_.refs_1_), channel_id=1, source_target_pairs={{0,8},{8,0},{16,24},{24,16},{1,9},{9,1},{17,25},{25,17},{2,10},{10... | collective-permute-start | bytes 737288 | tf_op jit(solution)/shard_map/ppermute | solution.py:1546
  169.9 11.2 %collective-permute-start.35 = (bf16[960,128]{1,0:T(8,128)(2,1)S(1)}, bf16[960,128]{1,0:T(8,128)(2,1)S(1)}, u32[]{:S(2)}, u32[]{:S(2)}) collective-permute-start(bf16[960,128]{1,0:T(8,128)(2,1)S(1)} %get-tuple-element.183.refs_9_.refs_1_), channel_id=1, source_target_pairs={{0,16},{8,24},{16,0},{24,8},{1,17},{9,25},{17,1},{25,9},{2,18},{10... | collective-permute-start | bytes 737288 | tf_op jit(solution)/shard_map/ppermute | solution.py:1546
  171.4 11.1 %collective-permute-start.36 = (bf16[960,128]{1,0:T(8,128)(2,1)S(1)}, bf16[960,128]{1,0:T(8,128)(2,1)S(1)}, u32[]{:S(2)}, u32[]{:S(2)}) collective-permute-start(bf16[960,128]{1,0:T(8,128)(2,1)S(1)} %get-tuple-element.183.refs_9_.refs_1_), channel_id=1, source_target_pairs={{0,24},{8,16},{16,8},{24,0},{1,25},{9,17},{17,9},{25,1},{2,26},{10... | collective-permute-start | bytes 737288 | tf_op jit(solution)/shard_map/ppermute | solution.py:1546
  (11 other events, 73.4 us)

commit v2 on v1

--- a/solution.py
+++ b/solution.py
@@ -207,36 +207,36 @@
 
 def attend_back(kaug, qa, v, kta, qm, doa, dom, delta, lse, dk, dv, dqt, heads):
     length = kaug.shape[0]
-    dk[...] = jnp.zeros_like(dk)
-    dv[...] = jnp.zeros_like(dv)
     slope_sums = [jnp.zeros((1, BQ), F32) for _ in range(heads)]
     for i in range(length // BQ):
         off = i * BQ
         here = slice(off, off + BQ)
-        for h in range(heads):
-            qh = qa[h, :, here]
-            doh = doa[h, :, here]
-            row_lse = lse[h : h + 1, here]
-            row_delta = delta[h : h + 1, here]
-            queries = qm[h, here, :]
-            grads = dom[h, here, :]
-            turned = None
-            for part in ((here, True),) + (((slice(0, off), False),) if off else ()):
-                span, masked = part
-                soft = jnp.exp(mm(kaug[span, :], qh) - row_lse)
+        turned = [None] * heads
+        for span, masked in ((here, True),) + (((slice(0, off), False),) if off else ()):
+            value_sum = key_sum = None
+            for h in range(heads):
+                soft = jnp.exp(mm(kaug[span, :], qa[h, :, here]) - lse[h : h + 1, here])
                 if masked:
                     soft = jnp.where(causal(), soft, 0.0)
-                score = (soft * (mm(v[span, :], doh) - row_delta)).astype(BF)
-                dv[span, :] += mm(soft.astype(BF), grads)
-                dk[span, :] += mm(score, queries)
+                score = (soft * (mm(v[span, :], doa[h, :, here]) - delta[h : h + 1, here])).astype(BF)
+                one, two = mm(soft.astype(BF), dom[h, here, :]), mm(score, qm[h, here, :])
+                value_sum = one if value_sum is None else value_sum + one
+                key_sum = two if key_sum is None else key_sum + two
                 more = mm(kta[h, :, span], score)
-                turned = more if turned is None else turned + more
-            dqt[HEAD * h : HEAD * h + HEAD, here] = turned[0:HEAD, :] * SCALE
-            spot = (off + iota((1, BQ), 1)).astype(F32)
+                turned[h] = more if turned[h] is None else turned[h] + more
+            if masked:
+                dv[span, :] = value_sum
+                dk[span, :] = key_sum
+            else:
+                dv[span, :] += value_sum
+                dk[span, :] += key_sum
+        spot = (off + iota((1, BQ), 1)).astype(F32)
+        for h in range(heads):
+            dqt[HEAD * h : HEAD * h + HEAD, here] = turned[h][0:HEAD, :] * SCALE
             slope_sums[h] = slope_sums[h] + (
-                turned[HEAD + 1 : HEAD + 2, :]
-                + turned[HEAD + 2 : HEAD + 3, :]
-                - spot * turned[HEAD : HEAD + 1, :]
+                turned[h][HEAD + 1 : HEAD + 2, :]
+                + turned[h][HEAD + 2 : HEAD + 3, :]
+                - spot * turned[h][HEAD : HEAD + 1, :]
             )
     return slope_sums
 
@@ -498,7 +498,30 @@
     return call(body, "pass_on", [array], [NEAR], [(array.shape, array.dtype)], after=after, weight=weight)[0]
 
 
-def first_rows(pieces, wq, lnp):
+def load_weights(weights):
+    def body(*refs):
+        sources, targets, semaphores = refs[: len(weights)], refs[len(weights) : -1], refs[-1]
+        loads = [
+            pltpu.make_async_copy(source if layer is None else source.at[layer], target.ref, semaphores.at[i])
+            for i, (source, target, (_, layer)) in enumerate(zip(sources, targets, weights))
+        ]
+        for load in loads:
+            load.start()
+        for load in loads:
+            load.wait()
+
+    return call(
+        body,
+        "load_weights",
+        [weight for weight, _ in weights],
+        [RAW] * len(weights),
+        [(weight.shape[-2:], BF, HOLD) for weight, _ in weights],
+        [pltpu.SemaphoreType.DMA((len(weights),))],
+        weight=100,
+    )
+
+
+def first_rows(pieces, wq, lnp, after):
     rows, d = pieces[0].shape
     width = wq.shape[1]
 
@@ -516,10 +539,10 @@
             qkv[here, :] = mm(attn[here, :], w_ref.get()[...]).astype(BF)
 
     outs = [((len(pieces) * rows, d), BF), ((len(pieces) * rows, width), BF)]
-    return call(body, "first_rows", [*pieces, wq, lnp], [NEAR] * len(pieces) + [ALL, NEAR], outs)
-
-
-def first_attention(idx, slopes, pieces, early, wq, lnp, weights, head_count, dh, after):
+    return call(body, "first_rows", [*pieces, wq, lnp], [NEAR] * len(pieces) + [ALL, NEAR], outs, after=after)
+
+
+def first_attention(idx, slopes, pieces, early, wq, lnp, head_count, dh, after):
     n = len(pieces)
     given = [k for k in range(n) if pieces[k] is not None]
     gone = [k for k in range(n) if pieces[k] is None]
@@ -532,18 +555,9 @@
         piece_refs = dict(zip(given, refs[2 : 2 + len(given)]))
         early_attn, early_qkv, w_ref, ln_ref = refs[2 + len(given) : 6 + len(given)]
         refs = refs[6 + len(given) :]
-        sources, refs = refs[: len(weights)], refs[len(weights) :]
         sends, refs = refs[:n], refs[n:]
-        attn, qkv, mixt, lse = refs[:4]
-        targets, refs = refs[4 : 4 + len(weights)], refs[4 + len(weights) :]
-        kaug, qa, vt, whole = refs[:4]
+        attn, qkv, mixt, lse, kaug, qa, vt, whole = refs
         s = idx_ref[0]
-        loads = [
-            pltpu.make_async_copy(source if layer is None else source.at[layer], target.ref, refs[4].at[i])
-            for i, (source, target, (_, layer)) in enumerate(zip(sources, targets, weights))
-        ]
-        for load in loads:
-            load.start()
         place_positions(kaug, width)
         gain, bias = ln_ref[0:1, :], ln_ref[4:5, :]
         own_weights = None
@@ -578,8 +592,6 @@
         whole[...] = flip(mixt.ref[...].astype(BF))
         for k in range(n):
             sends[k][...] = whole[rows_at((s ^ k) * rows, rows), 0:dh]
-        for load in loads:
-            load.wait()
 
     outs = [((rows, dh), BF)] * n + [
         ((length, d), BF, hold(n)),
@@ -587,22 +599,20 @@
         ((width, length), F32, hold(n)),
         ((8, length), F32, hold(n)),
     ]
-    outs += [(weight.shape[-2:], BF, HOLD) for weight, _ in weights]
     scratch = attend_scratch(length, width, head_count) + [
         pltpu.VMEM((width, length), BF),
         pltpu.VMEM((length, width), BF),
-        pltpu.SemaphoreType.DMA((max(len(weights), 1),)),
     ]
     result = call(
         body,
         "first_attention",
-        [idx, slopes, *[pieces[k] for k in given], *early, wq, lnp, *[in_hbm(weight) for weight, _ in weights]],
-        [smem(), smem()] + [NEAR] * (len(given) + 2) + [ALL, NEAR] + [pl.BlockSpec(memory_space=pltpu.HBM)] * len(weights),
+        [idx, slopes, *[pieces[k] for k in given], *early, wq, lnp],
+        [smem(), smem()] + [NEAR] * (len(given) + 2) + [ALL, NEAR],
         outs,
         scratch,
         after=after,
     )
-    return result[:n], result[n : n + 4], result[n + 4 :]
+    return result[:n], result[n:]
 
 
 CARRY = 16
@@ -1575,16 +1585,17 @@
     lnp = jnp.concatenate([ln_gain.reshape(4, d), ln_bias.reshape(4, d)], axis=0).astype(F32)
     columns = [lax.dynamic_slice(w_qkv, (0, 0, g * d + s * dh), (1, d, dh))[0] for g in range(3)]
     wq = jnp.concatenate([jnp.pad(c, ((0, 0), (0, width - dh))) for c in columns], axis=1)
-    early = first_rows([hid, hidden_parts[n - 1]], wq, lnp)
+    loaded = [w_out, w_in, w_back]
+    up_held, back_held = w_up, w_back
+    if keeps(n):
+        *loaded, up_held, back_held = load_weights([(w_out, 0), (w_in, 0), (w_back, 0), (w_up, None), (w_back, 1)])
+    early = first_rows([hid, hidden_parts[n - 1]], wq, lnp, loaded[:1])
     given = mask_rows(out_grad[0], start_flags[0][:, None], [*hidden_parts[1:], early[1]])
     given_parts = [swap(given, "seq", k) for k in range(1, n - 1)]
 
-    loaded = [(w_out, 0), (w_in, 0), (w_back, 0), (w_up, None), (w_back, 1)] if keeps(n) else []
-    sends, (attn, qkv, mixt, lse), loaded = first_attention(
-        idx, slopes, [None, *hidden_parts[1 : n - 1], None], early, wq, lnp, loaded, head_count, dh, [given]
-    )
-    fetched = loaded[3:]
-    loaded = loaded[:3] or [w_out, w_in, w_back]
+    sends, (attn, qkv, mixt, lse) = first_attention(
+        idx, slopes, [None, *hidden_parts[1 : n - 1], None], early, wq, lnp, head_count, dh, [given]
+    )
     mixes = exchange(sends, "seq")
     given = pass_on(given, [*mixes[1:], *given_parts])
     last_given = swap(given, "seq", n - 1)
@@ -1595,9 +1606,8 @@
     pooled_parts = gather(pooled, "seq")
     forward_other = swap(forward, "batch", 1)
     given_parts = [given] + given_parts + [last_given]
-    begun, up_held, back_held, short_weights = [], w_up, w_back, [w_qkv, w_out, w_in, w_pool]
+    begun, short_weights = [], [w_qkv, w_out, w_in, w_pool]
     if keeps(n):
-        up_held, back_held = fetched
         result = short_start(idx, given_parts, up_held, back_held, short_weights[:3], w_pool, [mid])
         begun, short_weights = result[:4], result[4:]
     block_out, full_grad, pair, keep, give, small_short = short_layer(
@@ -1670,21 +1680,28 @@
     def pieces(z):
         return [plane(z), [(keep, z * last_rows, last_rows), (last_other[2 * z // far], z % (far // 2) * last_rows, last_rows)]]
 
-    short_total, result_keep, result_give, *messages = fold(
+    result_keep, result_give = fold(
+        "last_near",
+        [(BF, [block for z in range(far) if z % 2 == odd for block in pieces(z)]) for odd in range(2)],
+        [keep],
+        weight=0,
+    )
+    short_total, *messages = fold(
         "short_total",
-        [(BF, [short_sum])]
-        + [(BF, [block for z in range(far) if z % 2 == odd for block in pieces(z)]) for odd in range(2)]
-        + [(BF, [[(sends[k], 0, sends[k].shape[0])], short_sum]) for k in range(1, n)],
-        [keep],
+        [(BF, [short_sum])] + [(BF, [[(sends[k], 0, sends[k].shape[0])], short_sum]) for k in range(1, n)],
+        [result_keep],
+        weight=100,
     )
     both, count = size + last_rows, far // 2
     other = swap(result_give, "batch", 2)
     messages = [swap(message, "seq", k + 1) for k, message in enumerate(messages)]
+    after = [short_total]
     while count > 1:
         blocks = [[(part, i * both, both) for part in (result_keep, other)] for i in range(count)]
         result_keep, result_give = fold(
             "last_plane",
             [(BF, [blocks[i] for i in range(count) if i % 2 == odd]) for odd in range(2)],
+            after,
             weight=0,
         )
         other = swap(result_give, "batch", 2 * far // count)

time: 189 us -> 185 us (0.979)
  starting transfers between devices: 46.3 us -> 44.3 us
    ppermute x37, starting transfers between devices: 46.3 us -> 44.3 us  [swap(): return lax.ppermute(array, axis, [(i, i ^ by) for i in range(count)])]
    pallas_call x19 -> x21, Pallas kernels: 91.9 us -> 93.1 us  [call(): pl.pallas_call(kernel, out_shape=[shape_of[kind](out[0], out[1]) for out,...]
  transfers between devices with their start and end apart: 37 -> 37, of which waited for: 15 -> 14; matrix products, arithmetic and copies ran while one was open for 3% -> 2% of each run, Pallas kernels for 46% -> 47%
where the time goes in v2:
time: 185 us; the launch traced here: 182 us
  Pallas kernels  93.1 us (50%)
  starting transfers between devices  44.3 us (24%)
  waiting for transfers between devices  39 us (21%)
  local copies, waits for them, and re-layouts  3.31 us (2%)
    pallas_call x21, Pallas kernels, call(): pl.pallas_call(kernel, out_shape=[shape_of[kind](out[0], out[1]) for out,...  93.1 us
    ppermute x37, starting transfers between devices, swap(): return lax.ppermute(array, axis, [(i, i ^ by) for i in range(count)])  44.3 us
    ppermute x37, waiting for transfers between devices, swap(): return lax.ppermute(array, axis, [(i, i ^ by) for i in range(count)])  39 us
  transfers between devices with their start and end apart: 37, of which 14 were waited for; matrix products, arithmetic and copies ran while one was open for 2% of the time, Pallas kernels for 47%

profile of v2, /device:TPU:0, one launch (start us, length us, event | category | flops | bytes accessed | tf_op | source)
XLA Modules:
  0.0 181.9 jit_solution(8660921691270472373)
XLA Ops:
  0.6 4.0 %collective-permute-start.2 = (bf16[384,512]{1,0:T(8,128)(2,1)}, bf16[384,512]{1,0:T(8,128)(2,1)S(1)}, u32[]{:S(2)}, u32[]{:S(2)}) collective-permute-start(bf16[384,512]{1,0:T(8,128)(2,1)} %bitcast.23), channel_id=1, source_target_pairs={{0,24},{8,16},{16,8},{24,0},{1,25},{9,17},{17,9},{25,1},{2,26},{10... | collective-permute-start | bytes 1179656 | tf_op jit(solution)/shard_map/ppermute | solution.py:1556
  9.4 3.6 %load_weights.1 = (bf16[512,512]{1,0:T(8,128)(2,1)S(1)}, bf16[512,2048]{1,0:T(8,128)(2,1)S(1)}, bf16[2048,512]{1,0:T(8,128)(2,1)S(1)}, bf16[512,1536]{1,0:T(8,128)(2,1)S(1)}, bf16[2048,512]{1,0:T(8,128)(2,1)S(1)}) custom-call(bf16[2,512,512]{2,1,0:T(8,128)(2,1)} %refs_8_.1, bf16[2,512,2048]{2,1,0:T(8,128)(2,1)} %refs_9_.1, bf16[2,2048,512]{2,1,0:T(8,128)(2,1)} %refs_4_.1, ...), custom_call_target="tpu_custom_call" | custom-call | flops 99999997952 | tf_op jit(solution)/shard_map/load_weights/pallas_call | solution.py:432
  13.0 1.8 collective-permute-done.2.refs_1_.refs_4_
  14.8 1.7 first_rows.1
  16.5 6.1 %collective-permute-done.refs_2_ = bf16[384,512]{1,0:T(8,128)(2,1)S(1)} collective-permute-done((bf16[384,512]{1,0:T(8,128)(2,1)}, bf16[384,512]{1,0:T(8,128)(2,1)S(1)}, u32[]{:S(2)}, u32[]{:S(2)}) %collective-permute-start) | collective-permute-done | bytes 393248 | tf_op jit(solution)/shard_map/ppermute | solution.py:1556
  22.9 1.6 collective-permute-start.6
  25.8 8.6 %first_attention.1 = (bf16[384,128]{1,0:T(8,128)(2,1)S(1)}, bf16[384,128]{1,0:T(8,128)(2,1)S(1)}, bf16[384,128]{1,0:T(8,128)(2,1)S(1)}, bf16[384,128]{1,0:T(8,12...) custom-call(s32[2]{0:T(128)S(1)} %pad_add_fusion.refs_0_, ...), custom_call_target="tpu_custom_call" | custom-call | flops 10000000000 | tf_op jit(solution)/shard_map/first_attention/pallas_call | solution.py:432
  35.7 2.3 %collective-permute-start.5 = (bf16[384,128]{1,0:T(8,128)(2,1)S(1)}, bf16[384,128]{1,0:T(8,128)(2,1)S(1)}, u32[]{:S(2)}, u32[]{:S(2)}) collective-permute-start(bf16[384,128]{1,0:T(8,128)(2,1)S(1)} %get-tuple-element.115), channel_id=1, source_target_pairs={{0,24},{8,16},{16,8},{24,0},{1,25},{9,17},{17,9},{25,1},{2,26},{10... | collective-permute-start | bytes 294920 | tf_op jit(solution)/shard_map/ppermute | solution.py:1556
  38.0 2.1 %collective-permute-done.3.refs_1_.refs_3_ = bf16[384,128]{1,0:T(8,128)(2,1)S(1)} collective-permute-done((bf16[384,128]{1,0:T(8,128)(2,1)S(1)}, bf16[384,128]{1,0:T(8,128)(2,1)S(1)}, u32[]{:S(2)}, u32[]{:S(2)}) %collective-permute-start.3) | collective-permute-done | bytes 98336 | tf_op jit(solution)/shard_map/ppermute | solution.py:1556
  41.3 2.3 %collective-permute-start.11 = (bf16[128,1536]{1,0:T(8,128)(2,1)S(1)}, bf16[128,1536]{1,0:T(8,128)(2,1)S(1)}, u32[]{:S(2)}, u32[]{:S(2)}) collective-permute-start(bf16[128,1536]{1,0:T(8,128)(2,1)S(1)} %pass_on.1.refs_14_.refs_1_), channel_id=1, source_target_pairs={{0,24},{8,16},{16,8},{24,0},{1,25},{9,17},{17,9},{25,1},{2,26},{10... | collective-permute-start | bytes 1179656 | tf_op jit(solution)/shard_map/ppermute | solution.py:1556
  43.6 6.2 %first_ffn.1 = (f32[128,1536]{1,0:T(8,128)S(1)}, bf16[144,512]{1,0:T(8,128)(2,1)S(1)}, f32[384,512]{1,0:T(8,128)S(1)}, bf16[512,3072]{1,0:T(8,128)(2,1)S(1)}, bf16[384,2048]{1,0:T(8,128)(2,1)S(1)}) custom-call(s32[2]{0:T(128)S(1)} %pad_add_fusion.refs_0_, bf16[384,512]{1,0:T(8,128)(2,1)} %bitcast.26, bf16[384,128]{1,0:T(8,128)(2,1)S(1)} %get-tuple-element.112.refs_2_, ...), custom_call_target="tpu_custom_call" | custom-call | flops 10000000000 | tf_op jit(solution)/shard_map/first_ffn/pallas_call | solution.py:432
  50.6 1.6 collective-permute-start.8
  53.4 4.1 %short_start.1 = (bf16[512,1536]{1,0:T(8,128)(2,1)S(1)}, f32[512,512]{1,0:T(8,128)S(1)}, bf16[512,512]{1,0:T(8,128)(2,1)S(1)}, bf16[512,2048]{1,0:T(8,128)(2,1)S...) custom-call(s32[2]{0:T(128)S(1)} %pad_add_fusion.refs_0_, ...), custom_call_target="tpu_custom_call" | custom-call | flops 99999997952 | tf_op jit(solution)/shard_map/short_start/pallas_call | solution.py:432
  58.2 38.1 %short_layer.1 = (bf16[384,512]{1,0:T(8,128)(2,1)}, f32[384,512]{1,0:T(8,128)S(1)}, bf16[2,512,512]{2,1,0:T(8,128)(2,1)S(1)}, bf16[4,960,128]{2,1,0:T(8,128)(2,1...) custom-call(s32[2]{0:T(128)S(1)} %pad_add_fusion.refs_0_, f32[2,8]{1,0:T(2,128)S(1)} %copy-done.2, ...), custom_call_target="tpu_custom_call" | custom-call | flops 10000000000 | tf_op jit(solution)/shard_map/short_layer/pallas_call | solution.py:432
  96.4 4.4 %first_ffn_back.1 = (bf16[768,128]{1,0:T(8,128)(2,1)S(1)}, bf16[768,128]{1,0:T(8,128)(2,1)S(1)}, bf16[768,128]{1,0:T(8,128)(2,1)S(1)}, bf16[768,128]{1,0:T(8,128...) custom-call(s32[2]{0:T(128)S(1)} %pad_add_fusion.refs_0_, ...), custom_call_target="tpu_custom_call" | custom-call | flops 10000000000 | tf_op jit(solution)/shard_map/first_ffn_back/pallas_call | solution.py:432
  104.9 3.7 %first_ffn_weights.1 = (bf16[2304,128]{1,0:T(8,128)(2,1)S(1)}, bf16[2304,128]{1,0:T(8,128)(2,1)S(1)}, bf16[2304,128]{1,0:T(8,128)(2,1)S(1)}, bf16[2304,128]{1,0:T(8,128)(2,1)S(1)}) custom-call(s32[2]{0:T(128)S(1)} %pad_add_fusion.refs_0_, bf16[512,3072]{1,0:T(8,128)(2,1)S(1)} %get-tuple-element.138.refs_4_.refs_1_, ...), custom_call_target="tpu_custom_call" | custom-call | flops 10000000000 | tf_op jit(solution)/shard_map/first_ffn_weights/pallas_call | solution.py:432
  108.9 1.6 collective-permute-start.20
  113.7 10.9 %first_attention_back.1 = (bf16[512,128]{1,0:T(8,128)(2,1)S(1)}, bf16[512,128]{1,0:T(8,128)(2,1)S(1)}, bf16[512,128]{1,0:T(8,128)(2,1)S(1)}, bf16[512,128]{1,0:T...) custom-call(s32[2]{0:T(128)S(1)} %pad_add_fusion.refs_0_, ...), custom_call_target="tpu_custom_call" | custom-call | flops 10000000000 | tf_op jit(solution)/shard_map/first_attention_back/pallas_call | solution.py:432
  125.5 1.5 collective-permute-start.24
  129.4 1.5 collective-permute-start.27
  130.9 2.7 %collective-permute-start.21 = (bf16[960,128]{1,0:T(8,128)(2,1)S(1)}, bf16[960,128]{1,0:T(8,128)(2,1)S(1)}, u32[]{:S(2)}, u32[]{:S(2)}) collective-permute-start(bf16[960,128]{1,0:T(8,128)(2,1)S(1)} %get-tuple-element.160), channel_id=1, source_target_pairs={{0,4},{1,5},{2,6},{3,7},{4,0},{5,1},{6,2},{7,3},{8,12},{9,13},{10,... | collective-permute-start | bytes 737288 | tf_op jit(solution)/shard_map/ppermute | solution.py:1556
  136.7 2.1 %collective-permute-done.22.refs_1_ = bf16[1152,128]{1,0:T(8,128)(2,1)S(1)} collective-permute-done((bf16[1152,128]{1,0:T(8,128)(2,1)S(1)}, bf16[1152,128]{1,0:T(8,128)(2,1)S(1)}, u32[]{:S(2)}, u32[]{:S(2)}) %collective-permute-start.22) | collective-permute-done | bytes 294944 | tf_op jit(solution)/shard_map/ppermute | solution.py:1556
  139.0 1.5 collective-permute-start.32
  145.5 6.8 %collective-permute-done.32.refs_1_ = bf16[1952,128]{1,0:T(8,128)(2,1)S(1)} collective-permute-done((bf16[1952,128]{1,0:T(8,128)(2,1)S(1)}, bf16[1952,128]{1,0:T(8,128)(2,1)S(1)}, u32[]{:S(2)}, u32[]{:S(2)}) %collective-permute-start.32) | collective-permute-done | bytes 499744 | tf_op jit(solution)/shard_map/ppermute | solution.py:1556
  152.3 1.6 collective-permute-start.33
  154.0 11.6 %collective-permute-done.33.refs_1_ = bf16[976,128]{1,0:T(8,128)(2,1)S(1)} collective-permute-done((bf16[976,128]{1,0:T(8,128)(2,1)S(1)}, bf16[976,128]{1,0:T(8,128)(2,1)S(1)}, u32[]{:S(2)}, u32[]{:S(2)}) %collective-permute-start.33) | collective-permute-done | bytes 249888 | tf_op jit(solution)/shard_map/ppermute | solution.py:1556
  165.6 1.5 collective-permute-start.34
  167.2 1.4 collective-permute-start.35
  169.2 4.2 %input_gradient.1.refs_6_ = f32[384,512]{1,0:T(8,128)} custom-call(s32[2]{0:T(128)S(1)} %pad_add_fusion.refs_0_, bf16[1152,128]{1,0:T(8,128)(2,1)S(1)} %get-tuple-element.153.refs_1_, bf16[2112,128]{1,0:T(8,128)(2,1)S(1)} %collective-permute-done.29.refs_2_, bf16[2112,128]{1,0:T(8,128)(2,1)S(1)} %collective-permute-done.30.refs_3_, ...), custom_call_target="tpu_custom_call" | custom-call | tf_op jit(solution)/shard_map/input_gradient/pallas_call | solution.py:432
  173.4 3.0 %finish_short.1 = (f32[2,192,512]{2,1,0:T(8,128)}, f32[2,64,512]{2,1,0:T(8,128)}, f32[2,512,256]{2,1,0:T(8,128)}, f32[2,64,2048]{2,1,0:T(8,128)}, f32[192,512]{1...) custom-call(s32[2]{0:T(128)S(1)} %pad_add_fusion.refs_0_, ...), custom_call_target="tpu_custom_call" | custom-call | tf_op jit(solution)/shard_map/finish_short/pallas_call | solution.py:432
  176.4 2.8 %collective-permute-done.35.refs_3_ = bf16[960,128]{1,0:T(8,128)(2,1)S(1)} collective-permute-done((bf16[960,128]{1,0:T(8,128)(2,1)S(1)}, bf16[960,128]{1,0:T(8,128)(2,1)S(1)}, u32[]{:S(2)}, u32[]{:S(2)}) %collective-permute-start.35) | collective-permute-done | bytes 245792 | tf_op jit(solution)/shard_map/ppermute | solution.py:1556
  179.3 2.3 %finish_first.1 = (f32[2,192,512]{2,1,0:T(8,128)}, f32[2,64,512]{2,1,0:T(8,128)}, f32[2,512,256]{2,1,0:T(8,128)}, f32[2,64,2048]{2,1,0:T(8,128)}, f32[64,1536]{1,0:T(8,128)}) custom-call(s32[2]{0:T(128)S(1)} %pad_add_fusion.refs_0_, ...), custom_call_target="tpu_custom_call", output_to_operand_aliasing={{0}: (5, {}), {1}: (6, {}), {2}: (7, {}), {3}: (8, {})} | custom-call | flops 10000000000 | tf_op jit(solution)/shard_map/finish_first/pallas_call | solution.py:432
  (92 shorter events, 31.4 us)
Async XLA Ops:
  0.6 14.2 %collective-permute-start.2 = (bf16[384,512]{1,0:T(8,128)(2,1)}, bf16[384,512]{1,0:T(8,128)(2,1)S(1)}, u32[]{:S(2)}, u32[]{:S(2)}) collective-permute-start(bf16[384,512]{1,0:T(8,128)(2,1)} %bitcast.23), channel_id=1, source_target_pairs={{0,24},{8,16},{16,8},{24,0},{1,25},{9,17},{17,9},{25,1},{2,26},{10... | collective-permute-start | bytes 1179656 | tf_op jit(solution)/shard_map/ppermute | solution.py:1556
  4.6 18.0 %collective-permute-start = (bf16[384,512]{1,0:T(8,128)(2,1)}, bf16[384,512]{1,0:T(8,128)(2,1)S(1)}, u32[]{:S(2)}, u32[]{:S(2)}) collective-permute-start(bf16[384,512]{1,0:T(8,128)(2,1)} %bitcast.24), channel_id=1, source_target_pairs={{0,8},{8,0},{16,24},{24,16},{1,9},{9,1},{17,25},{25,17},{2,10},{10... | collective-permute-start | bytes 1179656 | tf_op jit(solution)/shard_map/ppermute | solution.py:1556
  5.1 17.5 %collective-permute-start.1 = (bf16[384,512]{1,0:T(8,128)(2,1)}, bf16[384,512]{1,0:T(8,128)(2,1)S(1)}, u32[]{:S(2)}, u32[]{:S(2)}) collective-permute-start(bf16[384,512]{1,0:T(8,128)(2,1)} %bitcast.25), channel_id=1, source_target_pairs={{0,16},{8,24},{16,0},{24,8},{1,17},{9,25},{17,1},{25,9},{2,18},{10... | collective-permute-start | bytes 1179656 | tf_op jit(solution)/shard_map/ppermute | solution.py:1556
  22.9 18.4 %collective-permute-start.6 = (bf16[128,1536]{1,0:T(8,128)(2,1)S(1)}, bf16[128,1536]{1,0:T(8,128)(2,1)S(1)}, u32[]{:S(2)}, u32[]{:S(2)}) collective-permute-start(bf16[128,1536]{1,0:T(8,128)(2,1)S(1)} %mask_rows.1.refs_8_.refs_0_), channel_id=1, source_target_pairs={{0,8},{8,0},{16,24},{24,16},{1,9},{9,1},{17,25},{25,17},{2,10},{10... | collective-permute-start | bytes 1179656 | tf_op jit(solution)/shard_map/ppermute | solution.py:1556
  24.4 16.8 %collective-permute-start.7 = (bf16[128,1536]{1,0:T(8,128)(2,1)S(1)}, bf16[128,1536]{1,0:T(8,128)(2,1)S(1)}, u32[]{:S(2)}, u32[]{:S(2)}) collective-permute-start(bf16[128,1536]{1,0:T(8,128)(2,1)S(1)} %mask_rows.1.refs_8_.refs_0_), channel_id=1, source_target_pairs={{0,16},{8,24},{16,0},{24,8},{1,17},{9,25},{17,1},{25,9},{2,18},{10... | collective-permute-start | bytes 1179656 | tf_op jit(solution)/shard_map/ppermute | solution.py:1556
  35.0 6.2 %collective-permute-start.4 = (bf16[384,128]{1,0:T(8,128)(2,1)S(1)}, bf16[384,128]{1,0:T(8,128)(2,1)S(1)}, u32[]{:S(2)}, u32[]{:S(2)}) collective-permute-start(bf16[384,128]{1,0:T(8,128)(2,1)S(1)} %get-tuple-element.114), channel_id=1, source_target_pairs={{0,16},{8,24},{16,0},{24,8},{1,17},{9,25},{17,1},{25,9},{2,18},{10... | collective-permute-start | bytes 294920 | tf_op jit(solution)/shard_map/ppermute | solution.py:1556
  41.3 12.1 %collective-permute-start.11 = (bf16[128,1536]{1,0:T(8,128)(2,1)S(1)}, bf16[128,1536]{1,0:T(8,128)(2,1)S(1)}, u32[]{:S(2)}, u32[]{:S(2)}) collective-permute-start(bf16[128,1536]{1,0:T(8,128)(2,1)S(1)} %pass_on.1.refs_14_.refs_1_), channel_id=1, source_target_pairs={{0,24},{8,16},{16,8},{24,0},{1,25},{9,17},{17,9},{25,1},{2,26},{10... | collective-permute-start | bytes 1179656 | tf_op jit(solution)/shard_map/ppermute | solution.py:1556
  49.8 7.7 %collective-permute-start.10 = (bf16[144,512]{1,0:T(8,128)(2,1)S(1)}, bf16[144,512]{1,0:T(8,128)(2,1)S(1)}, u32[]{:S(2)}, u32[]{:S(2)}) collective-permute-start(bf16[144,512]{1,0:T(8,128)(2,1)S(1)} %get-tuple-element.118.refs_2_), channel_id=1, source_target_pairs={{0,24},{8,16},{16,8},{24,0},{1,25},{9,17},{17,9},{25,1},{2,26},{10... | collective-permute-start | bytes 442376 | tf_op jit(solution)/shard_map/ppermute | solution.py:1556
  50.6 7.7 %collective-permute-start.8 = (bf16[144,512]{1,0:T(8,128)(2,1)S(1)}, bf16[144,512]{1,0:T(8,128)(2,1)S(1)}, u32[]{:S(2)}, u32[]{:S(2)}) collective-permute-start(bf16[144,512]{1,0:T(8,128)(2,1)S(1)} %get-tuple-element.118.refs_2_), channel_id=1, source_target_pairs={{0,8},{8,0},{16,24},{24,16},{1,9},{9,1},{17,25},{25,17},{2,10},{10... | collective-permute-start | bytes 442376 | tf_op jit(solution)/shard_map/ppermute | solution.py:1556
  52.2 6.0 %collective-permute-start.9 = (bf16[144,512]{1,0:T(8,128)(2,1)S(1)}, bf16[144,512]{1,0:T(8,128)(2,1)S(1)}, u32[]{:S(2)}, u32[]{:S(2)}) collective-permute-start(bf16[144,512]{1,0:T(8,128)(2,1)S(1)} %get-tuple-element.118.refs_2_), channel_id=1, source_target_pairs={{0,16},{8,24},{16,0},{24,8},{1,17},{9,25},{17,1},{25,9},{2,18},{10... | collective-permute-start | bytes 442376 | tf_op jit(solution)/shard_map/ppermute | solution.py:1556
  53.4 43.0 %collective-permute-start.12 = (bf16[512,3072]{1,0:T(8,128)(2,1)S(1)}, bf16[512,3072]{1,0:T(8,128)(2,1)S(1)}, u32[]{:S(2)}, u32[]{:S(2)}) collective-permute-start(bf16[512,3072]{1,0:T(8,128)(2,1)S(1)} %get-tuple-element.138.refs_4_.refs_1_), channel_id=1, source_target_pairs={{0,1},{1,0},{2,3},{3,2},{4,5},{5,4},{6,7},{7,6},{8,9},{9,8},{10,11... | collective-permute-start | bytes 9437192 | tf_op jit(solution)/shard_map/ppermute | solution.py:1556
  100.9 7.7 %collective-permute-start.16 = (bf16[3840,128]{1,0:T(8,128)(2,1)S(1)}, bf16[3840,128]{1,0:T(8,128)(2,1)S(1)}, u32[]{:S(2)}, u32[]{:S(2)}) collective-permute-start(bf16[3840,128]{1,0:T(8,128)(2,1)S(1)} %bitcast.30), channel_id=1, source_target_pairs={{0,1},{1,0},{2,3},{3,2},{4,5},{5,4},{6,7},{7,6},{8,9},{9,8},{10,11... | collective-permute-start | bytes 2949128 | tf_op jit(solution)/shard_map/ppermute | solution.py:1556
  101.4 9.9 %collective-permute-start.13 = (bf16[768,128]{1,0:T(8,128)(2,1)S(1)}, bf16[768,128]{1,0:T(8,128)(2,1)S(1)}, u32[]{:S(2)}, u32[]{:S(2)}) collective-permute-start(bf16[768,128]{1,0:T(8,128)(2,1)S(1)} %get-tuple-element.140), channel_id=1, source_target_pairs={{0,8},{8,0},{16,24},{24,16},{1,9},{9,1},{17,25},{25,17},{2,10},{10... | collective-permute-start | bytes 589832 | tf_op jit(solution)/shard_map/ppermute | solution.py:1556
  102.1 10.6 %collective-permute-start.14 = (bf16[768,128]{1,0:T(8,128)(2,1)S(1)}, bf16[768,128]{1,0:T(8,128)(2,1)S(1)}, u32[]{:S(2)}, u32[]{:S(2)}) collective-permute-start(bf16[768,128]{1,0:T(8,128)(2,1)S(1)} %get-tuple-element.141), channel_id=1, source_target_pairs={{0,16},{8,24},{16,0},{24,8},{1,17},{9,25},{17,1},{25,9},{2,18},{10... | collective-permute-start | bytes 589832 | tf_op jit(solution)/shard_map/ppermute | solution.py:1556
  103.6 10.1 %collective-permute-start.15 = (bf16[768,128]{1,0:T(8,128)(2,1)S(1)}, bf16[768,128]{1,0:T(8,128)(2,1)S(1)}, u32[]{:S(2)}, u32[]{:S(2)}) collective-permute-start(bf16[768,128]{1,0:T(8,128)(2,1)S(1)} %get-tuple-element.142), channel_id=1, source_target_pairs={{0,24},{8,16},{16,8},{24,0},{1,25},{9,17},{17,9},{25,1},{2,26},{10... | collective-permute-start | bytes 589832 | tf_op jit(solution)/shard_map/ppermute | solution.py:1556
  108.9 18.1 %collective-permute-start.20 = (bf16[1920,128]{1,0:T(8,128)(2,1)S(1)}, bf16[1920,128]{1,0:T(8,128)(2,1)S(1)}, u32[]{:S(2)}, u32[]{:S(2)}) collective-permute-start(bf16[1920,128]{1,0:T(8,128)(2,1)S(1)} %get-tuple-element.157), channel_id=1, source_target_pairs={{0,2},{1,3},{2,0},{3,1},{4,6},{5,7},{6,4},{7,5},{8,10},{9,11},{10,... | collective-permute-start | bytes 1474568 | tf_op jit(solution)/shard_map/ppermute | solution.py:1556
  110.5 17.6 %collective-permute-start.18 = (bf16[2304,128]{1,0:T(8,128)(2,1)S(1)}, bf16[2304,128]{1,0:T(8,128)(2,1)S(1)}, u32[]{:S(2)}, u32[]{:S(2)}) collective-permute-start(bf16[2304,128]{1,0:T(8,128)(2,1)S(1)} %get-tuple-element.154), channel_id=1, source_target_pairs={{0,8},{8,0},{16,24},{24,16},{1,9},{9,1},{17,25},{25,17},{2,10},{10... | collective-permute-start | bytes 1769480 | tf_op jit(solution)/shard_map/ppermute | solution.py:1556
  111.3 16.8 %collective-permute-start.19 = (bf16[2304,128]{1,0:T(8,128)(2,1)S(1)}, bf16[2304,128]{1,0:T(8,128)(2,1)S(1)}, u32[]{:S(2)}, u32[]{:S(2)}) collective-permute-start(bf16[2304,128]{1,0:T(8,128)(2,1)S(1)} %get-tuple-element.156), channel_id=1, source_target_pairs={{0,16},{8,24},{16,0},{24,8},{1,17},{9,25},{17,1},{25,9},{2,18},{10... | collective-permute-start | bytes 1769480 | tf_op jit(solution)/shard_map/ppermute | solution.py:1556
  124.6 6.3 %collective-permute-start.23 = (bf16[512,128]{1,0:T(8,128)(2,1)S(1)}, bf16[512,128]{1,0:T(8,128)(2,1)S(1)}, u32[]{:S(2)}, u32[]{:S(2)}) collective-permute-start(bf16[512,128]{1,0:T(8,128)(2,1)S(1)} %get-tuple-element.166), channel_id=1, source_target_pairs={{0,8},{8,0},{16,24},{24,16},{1,9},{9,1},{17,25},{25,17},{2,10},{10... | collective-permute-start | bytes 393224 | tf_op jit(solution)/shard_map/ppermute | solution.py:1556
  125.5 8.1 %collective-permute-start.24 = (bf16[512,128]{1,0:T(8,128)(2,1)S(1)}, bf16[512,128]{1,0:T(8,128)(2,1)S(1)}, u32[]{:S(2)}, u32[]{:S(2)}) collective-permute-start(bf16[512,128]{1,0:T(8,128)(2,1)S(1)} %get-tuple-element.167), channel_id=1, source_target_pairs={{0,16},{8,24},{16,0},{24,8},{1,17},{9,25},{17,1},{25,9},{2,18},{10... | collective-permute-start | bytes 393224 | tf_op jit(solution)/shard_map/ppermute | solution.py:1556
  127.0 7.3 %collective-permute-start.25 = (bf16[512,128]{1,0:T(8,128)(2,1)S(1)}, bf16[512,128]{1,0:T(8,128)(2,1)S(1)}, u32[]{:S(2)}, u32[]{:S(2)}) collective-permute-start(bf16[512,128]{1,0:T(8,128)(2,1)S(1)} %get-tuple-element.168), channel_id=1, source_target_pairs={{0,24},{8,16},{16,8},{24,0},{1,25},{9,17},{17,9},{25,1},{2,26},{10... | collective-permute-start | bytes 393224 | tf_op jit(solution)/shard_map/ppermute | solution.py:1556
  128.5 10.2 %collective-permute-start.22 = (bf16[1152,128]{1,0:T(8,128)(2,1)S(1)}, bf16[1152,128]{1,0:T(8,128)(2,1)S(1)}, u32[]{:S(2)}, u32[]{:S(2)}) collective-permute-start(bf16[1152,128]{1,0:T(8,128)(2,1)S(1)} %get-tuple-element.165), channel_id=1, source_target_pairs={{0,16},{8,24},{16,0},{24,8},{1,17},{9,25},{17,1},{25,9},{2,18},{10... | collective-permute-start | bytes 884744 | tf_op jit(solution)/shard_map/ppermute | solution.py:1556
  129.4 9.3 %collective-permute-start.27 = (bf16[1152,128]{1,0:T(8,128)(2,1)S(1)}, bf16[1152,128]{1,0:T(8,128)(2,1)S(1)}, u32[]{:S(2)}, u32[]{:S(2)}) collective-permute-start(bf16[1152,128]{1,0:T(8,128)(2,1)S(1)} %get-tuple-element.173), channel_id=1, source_target_pairs={{0,8},{8,0},{16,24},{24,16},{1,9},{9,1},{17,25},{25,17},{2,10},{10... | collective-permute-start | bytes 884744 | tf_op jit(solution)/shard_map/ppermute | solution.py:1556
  130.9 10.7 %collective-permute-start.21 = (bf16[960,128]{1,0:T(8,128)(2,1)S(1)}, bf16[960,128]{1,0:T(8,128)(2,1)S(1)}, u32[]{:S(2)}, u32[]{:S(2)}) collective-permute-start(bf16[960,128]{1,0:T(8,128)(2,1)S(1)} %get-tuple-element.160), channel_id=1, source_target_pairs={{0,4},{1,5},{2,6},{3,7},{4,0},{5,1},{6,2},{7,3},{8,12},{9,13},{10,... | collective-permute-start | bytes 737288 | tf_op jit(solution)/shard_map/ppermute | solution.py:1556
  139.0 13.2 %collective-permute-start.32 = (bf16[1952,128]{1,0:T(8,128)(2,1)S(1)}, bf16[1952,128]{1,0:T(8,128)(2,1)S(1)}, u32[]{:S(2)}, u32[]{:S(2)}) collective-permute-start(bf16[1952,128]{1,0:T(8,128)(2,1)S(1)} %get-tuple-element.180), channel_id=1, source_target_pairs={{0,2},{1,3},{2,0},{3,1},{4,6},{5,7},{6,4},{7,5},{8,10},{9,11},{10,... | collective-permute-start | bytes 1499144 | tf_op jit(solution)/shard_map/ppermute | solution.py:1556
  141.9 26.7 %collective-permute-start.29 = (bf16[2112,128]{1,0:T(8,128)(2,1)S(1)}, bf16[2112,128]{1,0:T(8,128)(2,1)S(1)}, u32[]{:S(2)}, u32[]{:S(2)}) collective-permute-start(bf16[2112,128]{1,0:T(8,128)(2,1)S(1)} %get-tuple-element.176), channel_id=1, source_target_pairs={{0,8},{8,0},{16,24},{24,16},{1,9},{9,1},{17,25},{25,17},{2,10},{10... | collective-permute-start | bytes 1622024 | tf_op jit(solution)/shard_map/ppermute | solution.py:1556
  143.2 25.9 %collective-permute-start.30 = (bf16[2112,128]{1,0:T(8,128)(2,1)S(1)}, bf16[2112,128]{1,0:T(8,128)(2,1)S(1)}, u32[]{:S(2)}, u32[]{:S(2)}) collective-permute-start(bf16[2112,128]{1,0:T(8,128)(2,1)S(1)} %get-tuple-element.177), channel_id=1, source_target_pairs={{0,16},{8,24},{16,0},{24,8},{1,17},{9,25},{17,1},{25,9},{2,18},{10... | collective-permute-start | bytes 1622024 | tf_op jit(solution)/shard_map/ppermute | solution.py:1556
  144.6 24.6 %collective-permute-start.31 = (bf16[2112,128]{1,0:T(8,128)(2,1)S(1)}, bf16[2112,128]{1,0:T(8,128)(2,1)S(1)}, u32[]{:S(2)}, u32[]{:S(2)}) collective-permute-start(bf16[2112,128]{1,0:T(8,128)(2,1)S(1)} %get-tuple-element.178), channel_id=1, source_target_pairs={{0,24},{8,16},{16,8},{24,0},{1,25},{9,17},{17,9},{25,1},{2,26},{10... | collective-permute-start | bytes 1622024 | tf_op jit(solution)/shard_map/ppermute | solution.py:1556
  152.3 13.2 %collective-permute-start.33 = (bf16[976,128]{1,0:T(8,128)(2,1)S(1)}, bf16[976,128]{1,0:T(8,128)(2,1)S(1)}, u32[]{:S(2)}, u32[]{:S(2)}) collective-permute-start(bf16[976,128]{1,0:T(8,128)(2,1)S(1)} %get-tuple-element.183), channel_id=1, source_target_pairs={{0,4},{1,5},{2,6},{3,7},{4,0},{5,1},{6,2},{7,3},{8,12},{9,13},{10,... | collective-permute-start | bytes 749576 | tf_op jit(solution)/shard_map/ppermute | solution.py:1556
  165.6 10.8 %collective-permute-start.34 = (bf16[960,128]{1,0:T(8,128)(2,1)S(1)}, bf16[960,128]{1,0:T(8,128)(2,1)S(1)}, u32[]{:S(2)}, u32[]{:S(2)}) collective-permute-start(bf16[960,128]{1,0:T(8,128)(2,1)S(1)} %get-tuple-element.184.refs_9_.refs_1_), channel_id=1, source_target_pairs={{0,8},{8,0},{16,24},{24,16},{1,9},{9,1},{17,25},{25,17},{2,10},{10... | collective-permute-start | bytes 737288 | tf_op jit(solution)/shard_map/ppermute | solution.py:1556
  167.2 12.1 %collective-permute-start.35 = (bf16[960,128]{1,0:T(8,128)(2,1)S(1)}, bf16[960,128]{1,0:T(8,128)(2,1)S(1)}, u32[]{:S(2)}, u32[]{:S(2)}) collective-permute-start(bf16[960,128]{1,0:T(8,128)(2,1)S(1)} %get-tuple-element.184.refs_9_.refs_1_), channel_id=1, source_target_pairs={{0,16},{8,24},{16,0},{24,8},{1,17},{9,25},{17,1},{25,9},{2,18},{10... | collective-permute-start | bytes 737288 | tf_op jit(solution)/shard_map/ppermute | solution.py:1556
  168.6 10.7 %collective-permute-start.36 = (bf16[960,128]{1,0:T(8,128)(2,1)S(1)}, bf16[960,128]{1,0:T(8,128)(2,1)S(1)}, u32[]{:S(2)}, u32[]{:S(2)}) collective-permute-start(bf16[960,128]{1,0:T(8,128)(2,1)S(1)} %get-tuple-element.184.refs_9_.refs_1_), channel_id=1, source_target_pairs={{0,24},{8,16},{16,8},{24,0},{1,25},{9,17},{17,9},{25,1},{2,26},{10... | collective-permute-start | bytes 737288 | tf_op jit(solution)/shard_map/ppermute | solution.py:1556
  (14 other events, 87.0 us)
